TPU v7x, 128 devices: a whole 4x4x4 slice. The times are simulated.
128 devices in a mesh: pair: 8 (over z, core), ri: 16 (over y, x).
Axes of the slice: x: 4, y: 4, z: 4, core: 2. Of those that a mesh axis runs over, the one named last changes fastest.
Arguments:
- integrals: bfloat16 [128, 5, 144, 128, 128], P('pair', None, 'ri'), may hold values from -0.23632812 to 0.23632812
- lam_index: int32 [128, 5], P('pair'), may hold values from 0 to 127, as said below
- tile_count: int32 [128], P('pair'), may hold values from 1 to 5
- screen: int32 [128, 5], P('pair'), may hold values 0 or 1
- coefficients: bfloat16 [128, 16384], P(None, ('pair', 'ri')), may hold values from -0.52734375 to 0.52734375
- metric: bfloat16 [144, 144], replicated, may hold values from -0.5 to 0.5
Outputs:
- exchange: float32 [16384, 2048], P(('pair', 'ri'))
Inputs may be any that keep to these rules, and one draw needn't show every extreme that they name: `lam_index`: slot 0 of block b names b itself; the partners of one block are distinct and lie ahead of it, cyclically, within 128 blocks.
All inputs are finite; a program needn't handle non-finite values. No bound on the sum of `screen` on one device may be relied on, other than what follows from the above.
Results may differ from a plain program's by a relative error of at most 0.0022.
Values may be sent and summed in bfloat16 or wider, within the bound.
No kernel may reach another device: no remote copies, remote signals or barrier semaphores. Data moves between devices by JAX's collectives and lax.ppermute only.
A program may use at most 256 MiB of HBM per device.

v0:
```python
import jax
import jax.numpy as jnp
from jax import lax
from jax.sharding import PartitionSpec as P


def body(integrals, lam_index, tile_count, screen, coefficients, metric):
    block_size = integrals.shape[-1]
    slot_count = integrals.shape[1]
    occupied = coefficients.shape[0]
    all_coefs = lax.all_gather(coefficients, ("pair", "ri"), axis=1, tiled=True)
    blocks = all_coefs.reshape(occupied, all_coefs.shape[1] // block_size, block_size)
    slot_ids = jnp.arange(slot_count, dtype=jnp.int32)
    kept_slot = jnp.where(
        (slot_ids[None, :] < tile_count[:, None]) & (screen > 0), 1.0, 0.0
    ).astype(jnp.float32)
    picked = blocks[:, lam_index]
    picked = (picked.astype(jnp.float32) * kept_slot[None, :, :, None]).astype(jnp.bfloat16)
    fitted = jnp.einsum("bsqml,obsl->oqbm", integrals, picked, preferred_element_type=jnp.float32)
    fitted = fitted.astype(jnp.bfloat16)
    fitted = fitted.reshape(occupied, fitted.shape[1], fitted.shape[2] * block_size)
    factors = jnp.einsum(
        "pq,oqm->opm",
        metric,
        lax.all_to_all(fitted, "ri", split_axis=0, concat_axis=1, tiled=True),
        preferred_element_type=jnp.float32,
    ).astype(jnp.bfloat16)
    return lax.psum_scatter(
        jnp.einsum("opm,opn->mn", factors, factors, preferred_element_type=jnp.float32),
        "ri",
        scatter_dimension=0,
        tiled=True,
    )


def solution(mesh):
    placed = (
        P("pair", None, "ri", None, None),
        P("pair", None),
        P("pair"),
        P("pair", None),
        P(None, ("pair", "ri")),
        P(),
    )
    return jax.shard_map(
        body, mesh=mesh, in_specs=placed, out_specs=P(("pair", "ri"), None), check_vma=False
    )
```

profile of v0, /device:TPU:0, one launch (start us, length us, event | category | flops | bytes accessed | tf_op | source)
XLA Modules:
  0.0 377.0 jit_solution(9417543947511338457)
XLA Ops:
  6.5 0.0 copy-start
  6.5 0.0 all-gather.2.cloned.1.call-start
  6.5 1.5 copy.25
  8.0 0.0 all-gather.2.cloned.1.call-update
  8.1 0.0 reduce-scatter.2.cloned.1.call-start
  8.1 0.7 compare_select_fusion
  8.8 0.1 copy.26
  8.9 0.1 reshape.12
  9.0 0.7 fusion.16
  9.7 0.1 copy.28
  9.8 70.0 %all-gather.2.cloned.1.call-done = bf16[128,16384]{0,1:T(8,128)(2,1)} async-done(((bf16[128,128]{0,1:T(8,128)(2,1)}), bf16[128,16384]{0,1:T(8,128)(2,1)}) %all-gather.2.cloned.1.call-update) | async-done | bytes 4194320 | tf_op jit(solution)/shard_map/all_gather | solution.py:11
  79.8 6.4 %copy.27 = bf16[128,128,128]{2,0,1:T(8,128)(2,1)} copy(bf16[128,128,128]{0,2,1:T(8,128)(2,1)} %bitcast.40) | data formatting | bytes 8388608 | tf_op jit(solution)/shard_map/reshape | solution.py:12
  86.2 3.2 gather_fusion
  89.5 12.4 %fusion.1 = bf16[128,9,16,128]{0,3,1,2:T(8,128)(2,1)} fusion(bf16[16,5,9,128,128]{4,3,2,1,0:T(8,128)(2,1)} %param.6, bf16[16,5,128,128]{3,2,1,0:T(8,128)(2,1)S(1)} %bitcast.38, f32[16,5]{1,0:T(8,128)S(1)} %copy.28), kind=kOutput, calls=%fused_computation.5 | convolution fusion | flops 3026190336 | bytes 30933312 | tf_op jit(solution)/shard_map/bsqml,obsl->oqbm/dot_general | solution.py:19
  101.9 6.3 %copy.30 = bf16[128,9,16,128]{0,3,2,1:T(8,128)(2,1)} copy(bf16[128,9,16,128]{0,3,1,2:T(8,128)(2,1)} %fusion.1) | data formatting | bytes 9437184 | tf_op jit(solution)/shard_map/convert_element_type | solution.py:20
  108.3 11.6 %copy.31 = bf16[128,9,2048]{2,1,0:T(8,128)(2,1)} copy(bf16[128,9,2048]{0,2,1:T(8,128)(2,1)} %bitcast.37) | data formatting | bytes 9437184 | tf_op jit(solution)/shard_map/reshape | solution.py:21
  119.9 100.8 %all_to_all.18 = bf16[128,9,2048]{2,1,0:T(8,128)(2,1)S(1)} all-to-all(bf16[128,9,2048]{2,1,0:T(8,128)(2,1)} %copy.31), channel_id=1, replica_groups=mesh['pair'=8,'ri'=16] {'ri'}, dimensions={0} | all-to-all | bytes 9437184 | tf_op jit(solution)/shard_map/all_to_all | solution.py:25
  220.7 5.5 %copy.33 = bf16[8,16,9,2048]{3,0,2,1:T(8,128)(2,1)} copy(bf16[8,16,9,2048]{3,2,0,1:T(8,128)(2,1)S(1)} %bitcast.36) | data formatting | bytes 9437184 | tf_op jit(solution)/shard_map/all_to_all | solution.py:25
  226.2 0.0 copy-done
  226.2 37.4 %convolution_bitcast_fusion = f32[2048,2048]{1,0:T(8,128)} fusion(bf16[8,144,2048]{2,0,1:T(8,128)(2,1)} %bitcast.39, bf16[144,144]{1,0:T(8,128)(2,1)S(1)} %copy-done), kind=kOutput, calls=%fused_computation.2 | convolution fusion | flops 10345512960 | bytes 21537280 | tf_op jit(solution)/shard_map/opm,opn->mn/dot_general | solution.py:29
  263.6 0.0 copy-start.1
  263.6 0.0 reduce-scatter.2.cloned.1.call-update
  263.6 106.6 %reduce-scatter.2.cloned.1.call-done = f32[128,2048]{1,0:T(8,128)} async-done(((f32[2048,2048]{1,0:T(8,128)}), f32[128,2048]{1,0:T(8,128)}) %reduce-scatter.2.cloned.1.call-update) | async-done | bytes 1048592 | tf_op jit(solution)/shard_map/reduce_scatter | solution.py:28
  370.2 0.0 copy-done.1
  (1 shorter events, 0.0 us)
Async XLA Ops:
  6.5 219.6 %copy-start = (bf16[144,144]{1,0:T(8,128)(2,1)S(1)}, bf16[144,144]{1,0:T(8,128)(2,1)}, u32[]{:S(2)}) copy-start(bf16[144,144]{1,0:T(8,128)(2,1)} %param.11) | copy-start | bytes 124420
  6.5 73.3 %all-gather.2.cloned.1.call-start = ((), (), s32[]{:S(2)}) async-start(), calls=%async_computation.2 | async-start | bytes 4227072 | tf_op jit(solution)/shard_map/all_gather | solution.py:11
  8.1 362.1 %reduce-scatter.2.cloned.1.call-start = ((), (), s32[]{:S(2)}) async-start(), calls=%async_computation.3 | async-start | bytes 17825792 | tf_op jit(solution)/shard_map/reduce_scatter | solution.py:28
  263.6 106.6 %copy-start.1 = (bf16[144,144]{1,0:T(8,128)(2,1)S(1)}, bf16[144,144]{1,0:T(8,128)(2,1)}, u32[]{:S(2)}) copy-start(bf16[144,144]{1,0:T(8,128)(2,1)} %param.11) | copy-start | bytes 124420
Sparse Core Ops, SparseCore 0:
  10.5 69.2 all-gather.1
  263.7 106.4 reduce-scatter.1
where the time goes:
time: 378 us; the launch traced here: 377 us
  waiting for transfers between devices  177 us (47%)
  blocking collectives  101 us (27%)
  matrix products  49.8 us (13%)
  local copies, waits for them, and re-layouts  34.9 us (9%)
  between operations  13.4 us (4%)
    reduce_scatter x1, waiting for transfers between devices, body(): lax.psum_scatter(jnp.einsum('opm,opn->mn', factors, factors, preferred_el...  107 us
    all_to_all x1, blocking collectives, body(): lax.all_to_all(fitted, 'ri', split_axis=0, concat_axis=1, tiled=True)  101 us
    all_gather x1, waiting for transfers between devices, body(): all_coefs = lax.all_gather(coefficients, ('pair', 'ri'), axis=1, tiled=True)  70 us
    dot_general x1, matrix products, body(): jnp.einsum('opm,opn->mn', factors, factors, preferred_element_type=jnp.fl...  37.4 us
    dot_general x1, matrix products, body(): jnp.einsum('bsqml,obsl->oqbm', integrals, picked, preferred_element_type=...  12.4 us
    reshape x1, local copies, waits for them, and re-layouts, body(): fitted.reshape(occupied, fitted.shape[1], fitted.shape[2] * block_size)  11.6 us
  transfers between devices with their start and end apart: 2, of which 2 were waited for; matrix products, arithmetic and copies ran while one was open for 0% of the time, Pallas kernels for 0%

commit v1 on v0

v1 whole, which is shorter than its diff:
```python
import jax
import jax.numpy as jnp
from jax import lax
from jax.experimental import pallas as pl
from jax.experimental.pallas import tpu as pltpu
from jax.sharding import PartitionSpec as P

VMEM_LIMIT = 56 * 1024 * 1024
NT = (((1,), (1,)), ((), ()))


def fit_kernel(lam, kept, coefs, low_tiles, high_tiles, out, picked):
    slots, own_q, size = low_tiles.shape[1:4]
    ri = coefs.shape[0]
    owners, share = out.shape[0], out.shape[2] // 2
    step, steps = pl.program_id(0), pl.num_programs(0)
    for half, tiles in enumerate((low_tiles, high_tiles)):
        for s in range(slots):
            at = (step + half * steps) * slots + s
            block = lam[at]
            tile = coefs[lax.rem(block, ri), lax.div(block, ri)]
            picked[half, :, s * size:(s + 1) * size] = jnp.where(kept[at] > 0, tile, jnp.zeros_like(tile))
    for q in range(own_q):
        parts = []
        for half, tiles in enumerate((low_tiles, high_tiles)):
            wide = jnp.concatenate([tiles[0, s, q] for s in range(slots)], axis=1)
            value = lax.dot_general(picked[half], wide, NT, preferred_element_type=jnp.float32)
            parts.append(value.reshape(owners, share, size))
        out[:, q] = jnp.concatenate(parts, axis=1).astype(out.dtype)


def fit(integrals, lam, kept, coefs):
    blocks, slots, own_q, size, _ = integrals.shape
    occupied = coefs.shape[2]
    ri = coefs.shape[0]
    share = occupied // ri
    steps = blocks // 2
    tile_block = (1, slots, own_q, size, size)
    return pl.pallas_call(
        fit_kernel,
        grid_spec=pltpu.PrefetchScalarGridSpec(
            num_scalar_prefetch=2,
            grid=(steps,),
            in_specs=[
                pl.BlockSpec(coefs.shape, lambda i, *_: (0, 0, 0, 0)),
                pl.BlockSpec(tile_block, lambda i, *_: (i, 0, 0, 0, 0)),
                pl.BlockSpec(tile_block, lambda i, *_: (i + steps, 0, 0, 0, 0)),
            ],
            out_specs=pl.BlockSpec((ri, own_q, 2 * share, size), lambda i, *_: (0, 0, 0, i)),
            scratch_shapes=[pltpu.VMEM((2, occupied, slots * size), jnp.bfloat16)],
        ),
        out_shape=jax.ShapeDtypeStruct((ri, own_q, 2 * share, steps * size), jnp.bfloat16),
        compiler_params=pltpu.CompilerParams(vmem_limit_bytes=VMEM_LIMIT),
        name="fit",
    )(lam, kept, coefs, integrals, integrals)


def exchange_kernel(metric, fitted, out, wide, factors, turned):
    ri, own_q, rows, half_cols = fitted.shape
    share = rows // 2
    n_q = metric.shape[0]
    lanes = wide.shape[1]
    tile = wide.shape[3]
    chunk = lanes * tile
    size = out.shape[1]

    @pl.when(pl.program_id(0) == 0)
    def _():
        def one(c, _):
            base = pl.multiple_of(c * chunk, chunk)
            for k in range(own_q):
                x = fitted[:, k, :, pl.ds(base, chunk)].astype(jnp.float32)
                for h in range(2):
                    y = x[:, h * share:(h + 1) * share, :].reshape(ri * share, chunk)
                    for t in range(lanes):
                        wide[h, t, k * ri * share:(k + 1) * ri * share, :] = y[:, t * tile:(t + 1) * tile]
            for h in range(2):
                at = pl.multiple_of(base + h * half_cols, chunk)
                parts = []
                for o in range(share):
                    x = jnp.concatenate(
                        [wide[h, t, pl.ds(o, n_q, stride=share), :] for t in range(lanes)], axis=1
                    ).astype(jnp.bfloat16)
                    y = jnp.dot(metric[...], x, preferred_element_type=jnp.float32).astype(jnp.bfloat16)
                    parts.append(y)
                whole = jnp.concatenate(parts, axis=0)
                factors[:, pl.ds(at, chunk)] = whole
                if h == 0:
                    factors[:, pl.ds(pl.multiple_of(base + 2 * half_cols, chunk), chunk)] = whole
                turned[pl.ds(at, chunk), :] = whole.T
            return 0

        lax.fori_loop(0, half_cols // chunk, one, 0)

    pair = 2 * size
    span = out.shape[2]
    start = pl.multiple_of(pl.program_id(0) * pair, pair)
    value = jnp.dot(
        turned[pl.ds(start, pair), :],
        factors[:, pl.ds(start, span + size)],
        preferred_element_type=jnp.float32,
    ).astype(out.dtype)
    out[0] = value[:size, :span]
    out[1] = value[size:, size:]


def exchange_panels(metric, fitted):
    ri, own_q, rows, half_cols = fitted.shape
    cols = 2 * half_cols
    size = cols // ri
    span = (ri // 2 + 1) * size
    depth = own_q * ri * rows // 2
    return pl.pallas_call(
        exchange_kernel,
        grid=(ri // 2,),
        in_specs=[
            pl.BlockSpec(metric.shape, lambda i: (0, 0)),
            pl.BlockSpec(fitted.shape, lambda i: (0, 0, 0, 0)),
        ],
        out_specs=pl.BlockSpec((2, size, span), lambda i: (i, 0, 0)),
        out_shape=jax.ShapeDtypeStruct((ri, size, span), jnp.bfloat16),
        scratch_shapes=[
            pltpu.VMEM((2, 2, depth, size), jnp.float32),
            pltpu.VMEM((depth, cols + half_cols), jnp.bfloat16),
            pltpu.VMEM((cols, depth), jnp.bfloat16),
        ],
        compiler_params=pltpu.CompilerParams(vmem_limit_bytes=VMEM_LIMIT),
        name="exchange_panels",
    )(metric, fitted)


def sum_kernel(parts, own, mirror):
    total = parts[0].astype(jnp.float32)
    for s in range(1, parts.shape[0]):
        total = total + parts[s].astype(jnp.float32)
    own[...] = total
    mirror[0] = total.T.astype(mirror.dtype)


def sum_panels(parts):
    ri, size, span = parts.shape
    blocks = span // size
    return pl.pallas_call(
        sum_kernel,
        grid=(blocks,),
        in_specs=[pl.BlockSpec((ri, size, size), lambda d: (0, 0, d))],
        out_specs=[
            pl.BlockSpec((size, size), lambda d: (0, d)),
            pl.BlockSpec((1, size, size), lambda d: (d, 0, 0)),
        ],
        out_shape=[
            jax.ShapeDtypeStruct((size, span), jnp.float32),
            jax.ShapeDtypeStruct((blocks, size, size), jnp.bfloat16),
        ],
        name="sum_panels",
    )(parts)


def place_kernel(me, own, *rest):
    mirrors, out = rest[:-1], rest[-1]
    size = own.shape[0]
    ri = out.shape[1] // size
    for d in range(own.shape[1] // size):
        at = lax.rem(me[0] + d, ri) * size
        out[:, pl.ds(pl.multiple_of(at, size), size)] = own[:, d * size:(d + 1) * size]
    for d, mirror in enumerate(mirrors, 1):
        at = lax.rem(me[0] + ri - d, ri) * size
        out[:, pl.ds(pl.multiple_of(at, size), size)] = mirror[...].astype(out.dtype)


def place(me, own, mirrors):
    size = own.shape[0]
    ri = len(mirrors) * 2 + 2
    return pl.pallas_call(
        place_kernel,
        in_specs=[pl.BlockSpec(memory_space=pltpu.SMEM)] + [pl.BlockSpec(memory_space=pltpu.VMEM)] * (1 + len(mirrors)),
        out_specs=pl.BlockSpec(memory_space=pltpu.VMEM),
        out_shape=jax.ShapeDtypeStruct((size, ri * size), jnp.float32),
        name="place",
    )(me, own, *mirrors)


def body(integrals, lam_index, tile_count, screen, coefficients, metric):
    slots = integrals.shape[1]
    own_q = integrals.shape[2]
    ri = lax.axis_size("ri")
    slot_ids = jnp.arange(slots, dtype=jnp.int32)
    kept = ((slot_ids[None, :] < tile_count[:, None]) & (screen > 0)).astype(jnp.int32).reshape(-1)
    coefs = lax.all_gather(lax.all_gather(coefficients, "pair", axis=0), "ri", axis=0)
    mine = fit(integrals, lam_index.reshape(-1), kept, coefs)
    fitted = lax.all_to_all(mine, "ri", 0, 0)
    n_q = metric.shape[0]
    by_step = metric.reshape(n_q, ri, own_q).transpose(0, 2, 1).reshape(n_q, n_q)
    panels = exchange_panels(by_step, fitted)
    own, mirror = sum_panels(lax.all_to_all(panels, "ri", 0, 0))
    mirrors = [
        lax.ppermute(mirror[d], "ri", [(i, (i + d) % ri) for i in range(ri)])
        for d in range(1, ri // 2)
    ]
    me = lax.axis_index("ri").astype(jnp.int32).reshape(1)
    return place(me, own, mirrors)


def solution(mesh):
    placed = (
        P("pair", None, "ri", None, None),
        P("pair", None),
        P("pair"),
        P("pair", None),
        P(None, ("pair", "ri")),
        P(),
    )
    return jax.shard_map(
        body, mesh=mesh, in_specs=placed, out_specs=P(("pair", "ri"), None), check_vma=False
    )
```

time: 378 us -> 280 us (0.74)
  waiting for transfers between devices: 177 us -> 126 us
  matrix products: 49.8 us -> 0 us
  Pallas kernels: 0 us -> 41.5 us
  local copies, waits for them, and re-layouts: 34.9 us -> 4.51 us
  blocking collectives: 101 us -> 77.2 us
  starting transfers between devices: 0.04 us -> 14.9 us
    reduce_scatter x1 -> x0, waiting for transfers between devices: 107 us -> none  [body(): lax.psum_scatter(jnp.einsum('opm,opn->mn', factors, factors, preferred_el...]
    all_to_all x0 -> x1, waiting for transfers between devices: none -> 69.8 us  [body(): fitted = lax.all_to_all(mine, 'ri', 0, 0)]
    dot_general x2 -> x0, matrix products: 49.8 us -> none  [the longest x1 37.4 us: body(): jnp.einsum('opm,opn->mn', factors, factors, preferred_element_type=jnp.fl...]
    pallas_call x0 -> x4, Pallas kernels: none -> 41.5 us  [the longest x1 17.1 us: fit(): pl.pallas_call(fit_kernel, grid_spec=pltpu.PrefetchScalarGridSpec(num_sca...]
    all_to_all x1, blocking collectives: 101 us -> 61.8 us  [body(): own, mirror = sum_panels(lax.all_to_all(panels, 'ri', 0, 0))]
    all_gather x1, waiting for transfers between devices: 70 us -> 49.9 us  [body(): lax.all_gather(lax.all_gather(coefficients, 'pair', axis=0), 'ri', axis=0)]
    reshape x2 -> x5, local copies, waits for them, and re-layouts: 18 us -> 2.15 us  [the longest x2 0.78 us: body(): metric.reshape(n_q, ri, own_q).transpose(0, 2, 1).reshape(n_q, n_q)]
    all_gather x0 -> x1, blocking collectives: none -> 15.4 us  [body(): lax.all_gather(coefficients, 'pair', axis=0)]
  transfers between devices with their start and end apart: 2 -> 9, of which waited for: 2 -> 6; matrix products, arithmetic and copies ran while one was open for 0% -> 1% of each run, Pallas kernels for 0% -> 0%
where the time goes in v1:
time: 280 us; the launch traced here: 278 us
  waiting for transfers between devices  126 us (45%)
  blocking collectives  77.2 us (28%)
  Pallas kernels  41.5 us (15%)
  starting transfers between devices  14.9 us (5%)
  between operations  13.5 us (5%)
  local copies, waits for them, and re-layouts  4.51 us (2%)
    all_to_all x1, waiting for transfers between devices, body(): fitted = lax.all_to_all(mine, 'ri', 0, 0)  69.8 us
    all_to_all x1, blocking collectives, body(): own, mirror = sum_panels(lax.all_to_all(panels, 'ri', 0, 0))  61.8 us
    all_gather x1, waiting for transfers between devices, body(): lax.all_gather(lax.all_gather(coefficients, 'pair', axis=0), 'ri', axis=0)  49.9 us
    pallas_call x1, Pallas kernels, fit(): pl.pallas_call(fit_kernel, grid_spec=pltpu.PrefetchScalarGridSpec(num_sca...  17.1 us
    pallas_call x1, Pallas kernels, exchange_panels(): pl.pallas_call(exchange_kernel, grid=(ri // 2,), in_specs=[pl.BlockSpec(m...  15.4 us
    all_gather x1, blocking collectives, body(): lax.all_gather(coefficients, 'pair', axis=0)  15.4 us
    ppermute x7, starting transfers between devices, body(): lax.ppermute(mirror[d], 'ri', [(i, (i + d) % ri) for i in range(ri)])  9.5 us
    pallas_call x1, Pallas kernels, sum_panels(): pl.pallas_call(sum_kernel, grid=(blocks,), in_specs=[pl.BlockSpec((ri, si...  6.76 us
  transfers between devices with their start and end apart: 9, of which 6 were waited for; matrix products, arithmetic and copies ran while one was open for 1% of the time, Pallas kernels for 0%

profile of v1, /device:TPU:0, one launch (start us, length us, event | category | flops | bytes accessed | tf_op | source)
XLA Modules:
  0.0 278.3 jit_solution(13479751762310580232)
XLA Ops:
  6.5 15.4 %all-gather = bf16[1024,128]{1,0:T(8,128)(2,1)} all-gather(bf16[128,128]{1,0:T(8,128)(2,1)} %param.10), channel_id=2, replica_groups=mesh['pair'=8,'ri'=16] {'pair'}, dimensions={0}, use_global_device_ids=true | all-gather | bytes 294912 | tf_op jit(solution)/shard_map/all_gather | solution.py:189
  22.0 0.7 fusion.1
  22.7 0.7 reshape.25.kept
  23.4 0.8 copy.17
  24.2 0.6 reshape.21.lam
  24.8 49.9 %all-gather.4.cloned.1.call-done = bf16[128,128,128]{2,1,0:T(8,128)(2,1)} async-done(((bf16[8,128,128]{2,1,0:T(8,128)(2,1)}), bf16[128,128,128]{2,1,0:T(8,128)(2,1)}) %all-gather.4.cloned.1.call-update) | async-done | bytes 4194320 | tf_op jit(solution)/shard_map/all_gather | solution.py:189
  74.7 17.1 %fit.1 = bf16[16,9,16,1024]{3,2,1,0:T(8,128)(2,1)} custom-call(s32[80]{0:T(128)} %reshape.21.lam, s32[80]{0:T(128)} %reshape.25.kept, bf16[16,8,128,128]{3,2,1,0:T(8,128)(2,1)} %bitcast.21, bf16[16,5,9,128,128]{4,3,2,1,0:T(8,128)(2,1)} %high_tiles.1, bf16[16,5,9,128,128]{4,3,2,1,0:T(8,128)(2,1)} %high_tiles.1), custom_call_target="tpu_custom_call" | custom-call | tf_op jit(solution)/shard_map/fit/pallas_call | solution.py:39
  91.8 5.4 %all-to-all-start = ((bf16[16,9,16,1024]{3,2,1,0:T(8,128)(2,1)}), bf16[16,9,16,1024]{3,2,1,0:T(8,128)(2,1)}, u32[]{:S(2)}, u32[]{:S(2)}) async-start(bf16[16,9,16,1024]{3,2,1,0:T(8,128)(2,1)} %fit.1), calls=%async_computation | async-start | bytes 9437184 | tf_op jit(solution)/shard_map/all_to_all | solution.py:191
  97.5 0.7 copy.19.metric
  98.2 69.8 %all-to-all-done.fitted = bf16[16,9,16,1024]{3,2,1,0:T(8,128)(2,1)} async-done(((bf16[16,9,16,1024]{3,2,1,0:T(8,128)(2,1)}), bf16[16,9,16,1024]{3,2,1,0:T(8,128)(2,1)}, u32[]{:S(2)}, u32[]{:S(2)}) %all-to-all-start) | async-done | bytes 4718624 | tf_op jit(solution)/shard_map/all_to_all | solution.py:191
  168.0 15.4 %exchange_panels.1 = bf16[16,128,1152]{2,1,0:T(8,128)(2,1)} custom-call(bf16[144,144]{1,0:T(8,128)(2,1)} %copy.19.metric, bf16[16,9,16,1024]{3,2,1,0:T(8,128)(2,1)} %all-to-all-done.fitted), custom_call_target="tpu_custom_call" | custom-call | tf_op jit(solution)/shard_map/exchange_panels/pallas_call | solution.py:113
  183.4 61.8 %all_to_all.10.parts = bf16[16,128,1152]{2,1,0:T(8,128)(2,1)} all-to-all(bf16[16,128,1152]{2,1,0:T(8,128)(2,1)} %exchange_panels.1), channel_id=1, replica_groups=mesh['pair'=8,'ri'=16] {'ri'}, dimensions={0} | all-to-all | bytes 9437184 | tf_op jit(solution)/shard_map/all_to_all | solution.py:195
  245.2 6.8 %sum_panels.1 = (f32[128,1152]{1,0:T(8,128)}, bf16[9,128,128]{2,1,0:T(8,128)(2,1)}) custom-call(bf16[16,128,1152]{2,1,0:T(8,128)(2,1)} %all_to_all.10.parts), custom_call_target="tpu_custom_call" | custom-call | tf_op jit(solution)/shard_map/sum_panels/pallas_call | solution.py:143
  251.9 0.9 slice_bitcast_fusion
  252.8 1.1 collective-permute-start
  254.1 2.3 collective-permute-start.2
  256.4 0.9 collective-permute-start.3
  257.3 1.1 collective-permute-start.4
  258.4 2.1 collective-permute-done.rest_0_
  260.5 1.6 collective-permute-start.5
  262.1 2.3 collective-permute-start.6
  264.8 3.7 %collective-permute-done.5.rest_5_ = bf16[128,128]{1,0:T(8,128)(2,1)S(1)} collective-permute-done((bf16[128,128]{1,0:T(8,128)(2,1)S(1)}, bf16[128,128]{1,0:T(8,128)(2,1)S(1)}, u32[]{:S(2)}, u32[]{:S(2)}) %collective-permute-start.5) | collective-permute-done | bytes 32800 | tf_op jit(solution)/shard_map/ppermute | solution.py:197
  268.7 0.5 copy-done.6
  269.3 2.2 place.1
  (27 shorter events, 1.1 us)
Async XLA Ops:
  6.5 68.2 %all-gather.4.cloned.1.call-start = ((), (), s32[]{:S(2)}) async-start(), calls=%async_computation.2 | async-start | bytes 4456448 | tf_op jit(solution)/shard_map/all_gather | solution.py:189
  91.8 5.4 %copy-start = (bf16[144,144]{1,0:T(8,128)(2,1)S(1)}, bf16[144,144]{1,0:T(8,128)(2,1)}, u32[]{:S(2)}) copy-start(bf16[144,144]{1,0:T(8,128)(2,1)} %param.11) | copy-start | bytes 124420
  91.8 76.1 %all-to-all-start = ((bf16[16,9,16,1024]{3,2,1,0:T(8,128)(2,1)}), bf16[16,9,16,1024]{3,2,1,0:T(8,128)(2,1)}, u32[]{:S(2)}, u32[]{:S(2)}) async-start(bf16[16,9,16,1024]{3,2,1,0:T(8,128)(2,1)} %fit.1), calls=%async_computation | async-start | bytes 9437184 | tf_op jit(solution)/shard_map/all_to_all | solution.py:191
  252.8 7.7 %collective-permute-start = (bf16[128,128]{1,0:T(8,128)(2,1)S(1)}, bf16[128,128]{1,0:T(8,128)(2,1)S(1)}, u32[]{:S(2)}, u32[]{:S(2)}) collective-permute-start(bf16[128,128]{1,0:T(8,128)(2,1)S(1)} %get-tuple-element.15), channel_id=1, source_target_pairs={{0,1},{1,2},{2,3},{3,4},{4,5},{5,6},{6,7},{7,8},{8,9},{9,10},{10,1... | collective-permute-start | bytes 98312 | tf_op jit(solution)/shard_map/ppermute | solution.py:197
  253.9 8.2 %collective-permute-start.1 = (bf16[128,128]{1,0:T(8,128)(2,1)S(1)}, bf16[128,128]{1,0:T(8,128)(2,1)S(1)}, u32[]{:S(2)}, u32[]{:S(2)}) collective-permute-start(bf16[128,128]{1,0:T(8,128)(2,1)S(1)} %get-tuple-element.14), channel_id=1, source_target_pairs={{0,2},{1,3},{2,4},{3,5},{4,6},{5,7},{6,8},{7,9},{8,10},{9,11},{10,... | collective-permute-start | bytes 98312 | tf_op jit(solution)/shard_map/ppermute | solution.py:197
  254.1 10.3 %collective-permute-start.2 = (bf16[128,128]{1,0:T(8,128)(2,1)S(1)}, bf16[128,128]{1,0:T(8,128)(2,1)S(1)}, u32[]{:S(2)}, u32[]{:S(2)}) collective-permute-start(bf16[128,128]{1,0:T(8,128)(2,1)S(1)} %get-tuple-element.13), channel_id=1, source_target_pairs={{0,3},{1,4},{2,5},{3,6},{4,7},{5,8},{6,9},{7,10},{8,11},{9,12},{10... | collective-permute-start | bytes 98312 | tf_op jit(solution)/shard_map/ppermute | solution.py:197
  256.4 8.0 %collective-permute-start.3 = (bf16[128,128]{1,0:T(8,128)(2,1)S(1)}, bf16[128,128]{1,0:T(8,128)(2,1)S(1)}, u32[]{:S(2)}, u32[]{:S(2)}) collective-permute-start(bf16[128,128]{1,0:T(8,128)(2,1)S(1)} %get-tuple-element.12), channel_id=1, source_target_pairs={{0,4},{1,5},{2,6},{3,7},{4,8},{5,9},{6,10},{7,11},{8,12},{9,13},{1... | collective-permute-start | bytes 98312 | tf_op jit(solution)/shard_map/ppermute | solution.py:197
  257.3 7.5 %collective-permute-start.4 = (bf16[128,128]{1,0:T(8,128)(2,1)S(1)}, bf16[128,128]{1,0:T(8,128)(2,1)S(1)}, u32[]{:S(2)}, u32[]{:S(2)}) collective-permute-start(bf16[128,128]{1,0:T(8,128)(2,1)S(1)} %get-tuple-element.11), channel_id=1, source_target_pairs={{0,5},{1,6},{2,7},{3,8},{4,9},{5,10},{6,11},{7,12},{8,13},{9,14},{... | collective-permute-start | bytes 98312 | tf_op jit(solution)/shard_map/ppermute | solution.py:197
  260.5 8.2 %copy-start.1 = (bf16[128,128]{1,0:T(8,128)(2,1)}, bf16[128,128]{1,0:T(8,128)(2,1)S(1)}, u32[]{:S(2)}) copy-start(bf16[128,128]{1,0:T(8,128)(2,1)S(1)} %collective-permute-done.rest_0_) | copy-start | bytes 98308
  260.5 8.1 %collective-permute-start.5 = (bf16[128,128]{1,0:T(8,128)(2,1)S(1)}, bf16[128,128]{1,0:T(8,128)(2,1)S(1)}, u32[]{:S(2)}, u32[]{:S(2)}) collective-permute-start(bf16[128,128]{1,0:T(8,128)(2,1)S(1)} %get-tuple-element.10), channel_id=1, source_target_pairs={{0,6},{1,7},{2,8},{3,9},{4,10},{5,11},{6,12},{7,13},{8,14},{9,15},... | collective-permute-start | bytes 98312 | tf_op jit(solution)/shard_map/ppermute | solution.py:197
  262.1 6.6 %copy-start.2 = (bf16[128,128]{1,0:T(8,128)(2,1)}, bf16[128,128]{1,0:T(8,128)(2,1)S(1)}, u32[]{:S(2)}) copy-start(bf16[128,128]{1,0:T(8,128)(2,1)S(1)} %collective-permute-done.1.rest_1_) | copy-start | bytes 98308
  262.1 6.6 %collective-permute-start.6 = (bf16[128,128]{1,0:T(8,128)(2,1)S(1)}, bf16[128,128]{1,0:T(8,128)(2,1)S(1)}, u32[]{:S(2)}, u32[]{:S(2)}) collective-permute-start(bf16[128,128]{1,0:T(8,128)(2,1)S(1)} %get-tuple-element.9), channel_id=1, source_target_pairs={{0,7},{1,8},{2,9},{3,10},{4,11},{5,12},{6,13},{7,14},{8,15},{9,0},... | collective-permute-start | bytes 98312 | tf_op jit(solution)/shard_map/ppermute | solution.py:197
  264.4 4.3 %copy-start.3 = (bf16[128,128]{1,0:T(8,128)(2,1)}, bf16[128,128]{1,0:T(8,128)(2,1)S(1)}, u32[]{:S(2)}) copy-start(bf16[128,128]{1,0:T(8,128)(2,1)S(1)} %collective-permute-done.2.rest_2_) | copy-start | bytes 98308
  264.4 4.3 %copy-start.4 = (bf16[128,128]{1,0:T(8,128)(2,1)}, bf16[128,128]{1,0:T(8,128)(2,1)S(1)}, u32[]{:S(2)}) copy-start(bf16[128,128]{1,0:T(8,128)(2,1)S(1)} %collective-permute-done.3.rest_3_) | copy-start | bytes 98308
  264.8 3.9 %copy-start.5 = (bf16[128,128]{1,0:T(8,128)(2,1)}, bf16[128,128]{1,0:T(8,128)(2,1)S(1)}, u32[]{:S(2)}) copy-start(bf16[128,128]{1,0:T(8,128)(2,1)S(1)} %collective-permute-done.4.rest_4_) | copy-start | bytes 98308
  268.6 0.6 copy-start.6
  268.7 0.6 copy-start.7
Sparse Core Ops, SparseCore 0:
  22.1 52.5 all-gather.3

commit v2 on v0

v2 whole, which is shorter than its diff:
```python
import functools

import jax
import jax.numpy as jnp
from jax import lax
from jax.experimental import pallas as pl
from jax.experimental.pallas import tpu as pltpu
from jax.sharding import PartitionSpec as P

VMEM_LIMIT = 56 * 1024 * 1024
NT = (((1,), (1,)), ((), ()))
SIDE = 4
HALVES = 2
ON_VMEM = pl.BlockSpec(memory_space=pltpu.VMEM)
ON_SMEM = pl.BlockSpec(memory_space=pltpu.SMEM)


class Table:
    def __init__(self, blocks, slots):
        self.blocks, self.slots = blocks, slots
        self.count = 0
        self.pick = self.count + blocks
        self.row = self.pick + blocks * slots
        self.slot = self.row + blocks * slots
        self.ri = self.slot + blocks * slots
        self.x, self.y, self.core = self.ri + 1, self.ri + 2, self.ri + 3
        self.size = self.ri + 4


def prepare_kernel(at, place, lam, tile_count, screen, own, table, copies):
    for n in range(copies.shape[0]):
        copies[n] = own[...]
    for n in range(4):
        table[at.ri + n] = place[n]

    def one(b, _):
        count = jnp.int32(0)
        base = b * at.slots
        before = jnp.maximum(base - at.slots, 0)
        for s in range(at.slots):
            first = lax.rem(b, at.blocks // HALVES) == 0
            table[at.pick + base + s] = 0
            table[at.row + base + s] = jnp.where(first, b, table[at.row + before + s])
            table[at.slot + base + s] = jnp.where(first, s, table[at.slot + before + s])
        for s in range(at.slots):
            keep = jnp.logical_and(s < tile_count[b], screen[b, s] > 0)

            @pl.when(keep)
            def _():
                table[at.pick + base + count] = lam[b, s]
                table[at.row + base + count] = b
                table[at.slot + base + count] = s

            count = count + keep.astype(jnp.int32)
        table[at.count + b] = count
        return 0

    lax.fori_loop(0, at.blocks, one, 0)


def prepare(at, place, lam, tile_count, screen, own):
    return pl.pallas_call(
        functools.partial(prepare_kernel, at),
        in_specs=[ON_SMEM] * 4 + [ON_VMEM],
        out_specs=[ON_SMEM, ON_VMEM],
        out_shape=[
            jax.ShapeDtypeStruct((at.size,), jnp.int32),
            jax.ShapeDtypeStruct((SIDE,) + own.shape, own.dtype),
        ],
        name="prepare",
    )(place, lam, tile_count, screen, own)


def fit_kernel(at, table, same, other, *rest):
    slots = at.slots
    tiles, (out, picked, total) = rest[: HALVES * slots], rest[HALVES * slots:]
    ri = same.shape[0]
    own_q, size = out.shape[1], out.shape[3]
    share = out.shape[2] // HALVES
    step, steps = pl.program_id(0), pl.num_programs(0)
    for half in range(HALVES):
        block = step + half * steps
        count = table[at.count + block]

        @pl.when(count == 0)
        def _():
            total[half] = jnp.zeros(total.shape[1:], total.dtype)

        for s in range(0, slots, 2):
            pair = range(s, min(s + 2, slots))

            @pl.when(count > s)
            def _():
                for n, j in enumerate(pair):
                    name = table[at.pick + block * slots + j]
                    row, part = lax.rem(name, ri), lax.div(name, ri)
                    z, core = lax.div(part, 2), lax.rem(part, 2)
                    tile = jnp.where(core == table[at.core], same[row, z], other[row, z])
                    tile = jnp.where(j < count, tile, jnp.zeros_like(tile))
                    picked[half, :, n * size:(n + 1) * size] = tile
                depth = len(pair) * size
                wide = [tiles[half * slots + j][0, 0].reshape(own_q * size, size) for j in pair]
                wide = jnp.concatenate(wide, axis=1) if len(wide) > 1 else wide[0]
                value = lax.dot_general(picked[half, :, :depth], wide, NT, preferred_element_type=jnp.float32)
                total[half] = value if s == 0 else total[half] + value

    for q in range(own_q):
        parts = [
            total[half, :, q * size:(q + 1) * size].reshape(ri, share, size) for half in range(HALVES)
        ]
        out[:, q] = jnp.concatenate(parts, axis=1).astype(out.dtype)


def fit(at, table, integrals, same, other):
    blocks, slots, own_q, size, _ = integrals.shape
    ri, _, occupied, _ = same.shape
    share = occupied // ri
    steps = blocks // HALVES

    def place(half, j):
        def index(i, table):
            n = (i + half * steps) * slots + j
            return table[at.row + n], table[at.slot + n], 0, 0, 0

        return pl.BlockSpec((1, 1, own_q, size, size), index)

    whole = pl.BlockSpec(same.shape, lambda i, table: (0, 0, 0, 0))
    return pl.pallas_call(
        functools.partial(fit_kernel, at),
        grid_spec=pltpu.PrefetchScalarGridSpec(
            num_scalar_prefetch=1,
            grid=(steps,),
            in_specs=[whole, whole] + [place(half, j) for half in range(HALVES) for j in range(slots)],
            out_specs=pl.BlockSpec((ri, own_q, HALVES * share, size), lambda i, table: (0, 0, 0, i)),
            scratch_shapes=[
                pltpu.VMEM((HALVES, occupied, 2 * size), jnp.bfloat16),
                pltpu.VMEM((HALVES, occupied, own_q * size), jnp.float32),
            ],
        ),
        out_shape=jax.ShapeDtypeStruct((ri, own_q, HALVES * share, steps * size), jnp.bfloat16),
        compiler_params=pltpu.CompilerParams(vmem_limit_bytes=VMEM_LIMIT),
        name="fit",
    )(table, same, other, *[integrals] * (HALVES * slots))


def exchange_kernel(at, table, metric, fitted, *rest):
    by_x, by_y = rest[:SIDE], rest[SIDE:2 * SIDE]
    wide, factors, turned = rest[2 * SIDE:]
    ri, own_q, rows, half_cols = fitted.shape
    share = rows // HALVES
    n_q = metric.shape[0]
    lanes, tile = wide.shape[1], wide.shape[3]
    chunk = lanes * tile

    def one(c, _):
        base = pl.multiple_of(c * chunk, chunk)
        for k in range(own_q):
            x = fitted[:, k, :, pl.ds(base, chunk)].astype(jnp.float32)
            for r in range(ri):
                to = (r * own_q + k) * share
                for h in range(HALVES):
                    for t in range(lanes):
                        wide[h, t, to:to + share, :] = x[r, h * share:(h + 1) * share, t * tile:(t + 1) * tile]
        for h in range(HALVES):
            start = pl.multiple_of(base + h * half_cols, chunk)
            parts = []
            for o in range(share):
                x = jnp.concatenate(
                    [wide[h, t, pl.ds(o, n_q, stride=share), :] for t in range(lanes)], axis=1
                ).astype(jnp.bfloat16)
                parts.append(jnp.dot(metric[...], x, preferred_element_type=jnp.float32).astype(jnp.bfloat16))
            whole = jnp.concatenate(parts, axis=0)
            factors[:, pl.ds(start, chunk)] = whole
            if h == 0:
                factors[:, pl.ds(pl.multiple_of(base + HALVES * half_cols, chunk), chunk)] = whole
            turned[pl.ds(start, chunk), :] = whole.T
        return 0

    lax.fori_loop(0, half_cols // chunk, one, 0)

    _, cut, span = by_x[0].shape
    size = 2 * cut

    def panels(n, _):
        start = pl.multiple_of(n * 2 * size, 2 * size)
        value = jnp.dot(
            turned[pl.ds(start, 2 * size), :],
            factors[:, pl.ds(start, span + size)],
            preferred_element_type=jnp.float32,
        ).astype(jnp.bfloat16)
        y = lax.div(n, SIDE // 2)
        for side in range(2):
            x = 2 * lax.rem(n, SIDE // 2) + side
            panel = value[side * size:(side + 1) * size, side * size:side * size + span]
            step_x = lax.rem(x + SIDE - table[at.x], SIDE)
            step_y = lax.rem(y + SIDE - table[at.y], SIDE)
            for k in range(SIDE):
                @pl.when(step_x == k)
                def _():
                    by_x[k][y] = panel[:cut]

                @pl.when(step_y == k)
                def _():
                    by_y[k][x] = panel[cut:]
        return 0

    lax.fori_loop(0, ri // 2, panels, 0)


def exchange_panels(at, table, metric, fitted):
    ri, own_q, rows, half_cols = fitted.shape
    cols = HALVES * half_cols
    size = cols // ri
    span = (ri // 2 + 1) * size
    depth = own_q * ri * rows // HALVES
    return pl.pallas_call(
        functools.partial(exchange_kernel, at),
        in_specs=[ON_SMEM, ON_VMEM, ON_VMEM],
        out_specs=[ON_VMEM] * (2 * SIDE),
        out_shape=[jax.ShapeDtypeStruct((SIDE, size // 2, span), jnp.bfloat16)] * (2 * SIDE),
        scratch_shapes=[
            pltpu.VMEM((HALVES, 2, depth, size), jnp.float32),
            pltpu.VMEM((depth, cols + half_cols), jnp.bfloat16),
            pltpu.VMEM((cols, depth), jnp.bfloat16),
        ],
        compiler_params=pltpu.CompilerParams(vmem_limit_bytes=VMEM_LIMIT),
        name="exchange_panels",
    )(table, metric, fitted)


def first_sum_kernel(at, table, *rest):
    ins, outs = rest[:2 * SIDE], rest[2 * SIDE:]
    for path, mine in enumerate((table[at.y], table[at.x])):
        for k in range(SIDE):
            to = lax.rem(mine + k, SIDE)
            total = ins[path * SIDE][to].astype(jnp.float32)
            for j in range(1, SIDE):
                total = total + ins[path * SIDE + j][to].astype(jnp.float32)
            out = outs[path * SIDE + k]
            out[...] = total.astype(out.dtype)


def first_sum(at, table, parts):
    shape = parts[0].shape[1:]
    return pl.pallas_call(
        functools.partial(first_sum_kernel, at),
        in_specs=[ON_SMEM] + [ON_VMEM] * len(parts),
        out_specs=[ON_VMEM] * len(parts),
        out_shape=[
            jax.ShapeDtypeStruct(shape, jnp.float32 if n % SIDE == 0 else jnp.bfloat16)
            for n in range(len(parts))
        ],
        compiler_params=pltpu.CompilerParams(vmem_limit_bytes=VMEM_LIMIT),
        name="first_sum",
    )(table, *parts)


def second_sum_kernel(*refs):
    ins, own, mirrors = refs[:2 * SIDE], refs[2 * SIDE], refs[2 * SIDE + 1:]
    cut = ins[0].shape[0]
    size = 2 * cut
    for path in range(2):
        total = ins[path * SIDE][...]
        for j in range(1, SIDE):
            total = total + ins[path * SIDE + j][...].astype(jnp.float32)
        own[path * cut:(path + 1) * cut, :] = total
    for d, mirror in enumerate(mirrors, 1):
        mirror[...] = own[:, d * size:(d + 1) * size].T.astype(mirror.dtype)


def second_sum(parts):
    cut, span = parts[0].shape
    size = 2 * cut
    mirrors = span // size - 2
    return pl.pallas_call(
        second_sum_kernel,
        in_specs=[ON_VMEM] * len(parts),
        out_specs=[ON_VMEM] * (1 + mirrors),
        out_shape=[jax.ShapeDtypeStruct((size, span), jnp.float32)]
        + [jax.ShapeDtypeStruct((size, size), jnp.bfloat16)] * mirrors,
        compiler_params=pltpu.CompilerParams(vmem_limit_bytes=VMEM_LIMIT),
        name="second_sum",
    )(*parts)


def place_kernel(at, table, own, *rest):
    mirrors, out = rest[:-1], rest[-1]
    size = own.shape[0]
    ri = out.shape[1] // size
    for d in range(own.shape[1] // size):
        to = lax.rem(table[at.ri] + d, ri) * size
        out[:, pl.ds(pl.multiple_of(to, size), size)] = own[:, d * size:(d + 1) * size]
    for d, mirror in enumerate(mirrors, 1):
        to = lax.rem(table[at.ri] + ri - d, ri) * size
        out[:, pl.ds(pl.multiple_of(to, size), size)] = mirror[...].astype(out.dtype)


def place_blocks(at, table, own, mirrors):
    size = own.shape[0]
    ri = len(mirrors) * 2 + 2
    return pl.pallas_call(
        functools.partial(place_kernel, at),
        in_specs=[ON_SMEM] + [ON_VMEM] * (1 + len(mirrors)),
        out_specs=ON_VMEM,
        out_shape=jax.ShapeDtypeStruct((size, ri * size), jnp.float32),
        name="place_blocks",
    )(table, own, *mirrors)


def along_x(k):
    return [(y * SIDE + x, y * SIDE + (x + k) % SIDE) for y in range(SIDE) for x in range(SIDE)]


def along_y(k):
    return [(y * SIDE + x, (y + k) % SIDE * SIDE + x) for y in range(SIDE) for x in range(SIDE)]


def body(integrals, lam_index, tile_count, screen, coefficients, metric):
    ri, pairs = lax.axis_size("ri"), lax.axis_size("pair")
    at = Table(*integrals.shape[:2])
    here = lax.axis_index("ri").astype(jnp.int32)
    core = lax.rem(lax.axis_index("pair").astype(jnp.int32), 2)
    place = jnp.stack([here, lax.rem(here, SIDE), lax.div(here, SIDE), core])
    table, copies = prepare(at, place, lam_index, tile_count, screen, coefficients)

    one_core = [list(range(c, pairs, 2)) for c in range(2)]
    column = lax.all_to_all(copies, "pair", 0, 0, axis_index_groups=one_core, tiled=True)
    column = jnp.broadcast_to(column[None], (ri,) + column.shape)
    same = lax.all_to_all(column, "ri", 0, 0, tiled=True)
    other = lax.ppermute(same, "pair", [(p, p ^ 1) for p in range(pairs)])

    mine = fit(at, table, integrals, same, other)
    fitted = lax.all_to_all(mine, "ri", 0, 0, tiled=True)
    panels = exchange_panels(at, table, metric, fitted)

    def exchange_two(parts, first, second):
        return (
            parts[:1] + [lax.ppermute(parts[k], "ri", first(k)) for k in range(1, SIDE)]
            + parts[SIDE:SIDE + 1] + [lax.ppermute(parts[SIDE + k], "ri", second(k)) for k in range(1, SIDE)]
        )

    sums = first_sum(at, table, exchange_two(list(panels), along_x, along_y))
    own, *mirrors = second_sum(exchange_two(list(sums), along_y, along_x))
    mirrors = [
        lax.ppermute(mirror, "ri", [(i, (i + d) % ri) for i in range(ri)])
        for d, mirror in enumerate(mirrors, 1)
    ]
    return place_blocks(at, table, own, mirrors)


def solution(mesh):
    placed = (
        P("pair", None, "ri", None, None),
        P("pair", None),
        P("pair"),
        P("pair", None),
        P(None, ("pair", "ri")),
        P(),
    )
    return jax.shard_map(
        body, mesh=mesh, in_specs=placed, out_specs=P(("pair", "ri"), None), check_vma=False
    )
```

time: 378 us -> 238 us (0.63); the launches traced: 377 us -> 233 us
  waiting for transfers between devices: 177 us -> 47.8 us
  matrix products: 49.8 us -> 0 us
  Pallas kernels: 0 us -> 44 us
  local copies, waits for them, and re-layouts: 34.9 us -> 6.56 us
  starting transfers between devices: 0.04 us -> 25.3 us
  between operations: 13.4 us -> 0.15 us
  blocking collectives: 101 us -> 109 us
    reduce_scatter x1 -> x0, waiting for transfers between devices: 107 us -> none  [body(): lax.psum_scatter(jnp.einsum('opm,opn->mn', factors, factors, preferred_el...]
    all_gather x1 -> x0, waiting for transfers between devices: 70 us -> none  [body(): all_coefs = lax.all_gather(coefficients, ('pair', 'ri'), axis=1, tiled=True)]
    dot_general x2 -> x0, matrix products: 49.8 us -> none  [the longest x1 37.4 us: body(): jnp.einsum('opm,opn->mn', factors, factors, preferred_element_type=jnp.fl...]
    ppermute x0 -> x20, waiting for transfers between devices: none -> 47.8 us  [the longest x6 26.8 us: exchange_two(): lax.ppermute(parts[k], 'ri', first(k))]
    pallas_call x0 -> x6, Pallas kernels: none -> 44 us  [the longest x1 17.7 us: exchange_panels(): pl.pallas_call(functools.partial(exchange_kernel, at), in_specs=[ON_SMEM,...]
    ppermute x0 -> x20, starting transfers between devices: none -> 25.3 us  [the longest x7 13.5 us: body(): lax.ppermute(mirror, 'ri', [(i, (i + d) % ri) for i in range(ri)])]
    reshape x2 -> x0, local copies, waits for them, and re-layouts: 18 us -> none  [the longest x1 11.6 us: body(): fitted.reshape(occupied, fitted.shape[1], fitted.shape[2] * block_size)]
    all_to_all x1 -> x3, blocking collectives: 101 us -> 109 us  [the longest x1 62.4 us: body(): fitted = lax.all_to_all(mine, 'ri', 0, 0, tiled=True)]
  transfers between devices with their start and end apart: 2 -> 20, of which waited for: 2 -> 12; matrix products, arithmetic and copies ran while one was open for 0% -> 0% of each run, Pallas kernels for 0% -> 0%
where the time goes in v2:
time: 238 us; the launch traced here: 233 us
  blocking collectives  109 us (46%)
  waiting for transfers between devices  47.8 us (20%)
  Pallas kernels  44 us (18%)
  starting transfers between devices  25.3 us (11%)
  local copies, waits for them, and re-layouts  6.56 us (3%)
    all_to_all x1, blocking collectives, body(): fitted = lax.all_to_all(mine, 'ri', 0, 0, tiled=True)  62.4 us
    all_to_all x1, blocking collectives, body(): same = lax.all_to_all(column, 'ri', 0, 0, tiled=True)  34.8 us
    ppermute x6, waiting for transfers between devices, exchange_two(): lax.ppermute(parts[k], 'ri', first(k))  26.8 us
    pallas_call x1, Pallas kernels, exchange_panels(): pl.pallas_call(functools.partial(exchange_kernel, at), in_specs=[ON_SMEM,...  17.7 us
    pallas_call x1, Pallas kernels, fit(): pl.pallas_call(functools.partial(fit_kernel, at), grid_spec=pltpu.Prefetc...  15.3 us
    ppermute x7, starting transfers between devices, body(): lax.ppermute(mirror, 'ri', [(i, (i + d) % ri) for i in range(ri)])  13.5 us
    ppermute x6, waiting for transfers between devices, exchange_two(): lax.ppermute(parts[SIDE + k], 'ri', second(k))  13.1 us
    all_to_all x1, blocking collectives, body(): lax.all_to_all(copies, 'pair', 0, 0, axis_index_groups=one_core, tiled=True)  11.4 us
  transfers between devices with their start and end apart: 20, of which 12 were waited for; matrix products, arithmetic and copies ran while one was open for 0% of the time, Pallas kernels for 0%

profile of v2, /device:TPU:0, one launch (start us, length us, event | category | flops | bytes accessed | tf_op | source)
XLA Modules:
  0.0 233.0 jit_solution(7611406290397551789)
XLA Ops:
  3.3 2.6 %prepare.1 = (s32[260]{0:T(512)}, bf16[4,128,128]{2,1,0:T(8,128)(2,1)}) custom-call(s32[4]{0:T(128)} %pad_add_fusion.place, s32[16,5]{1,0:T(8,128)} %copy.7.lam, s32[16]{0:T(128)} %tile_count.1, s32[16,5]{1,0:T(8,128)} %copy.8.screen, bf16[128,128]{1,0:T(8,128)(2,1)} %own.1), custom_call_target="tpu_custom_call" | custom-call | tf_op jit(solution)/shard_map/prepare/pallas_call | solution.py:62
  5.9 11.4 %all_to_all.15 = bf16[4,128,128]{2,1,0:T(8,128)(2,1)S(1)} all-to-all(bf16[4,128,128]{2,1,0:T(8,128)(2,1)} %get-tuple-element.32), channel_id=1, replica_groups={{0,32,64,96},{16,48,80,112},{1,33,65,97},{17,49,81,113},{2,34,66,98},{1..., dimensions={0} | all-to-all | bytes 262144 | tf_op jit(solution)/shard_map/all_to_all | solution.py:327
  17.7 34.8 %all_to_all.16.same = bf16[16,4,128,128]{3,2,1,0:T(8,128)(2,1)S(1)} all-to-all(bf16[16,4,128,128]{3,2,1,0:T(8,128)(2,1)S(1)} %broadcast_in_dim.2), channel_id=1, replica_groups=mesh['pair'=8,'ri'=16] {'ri'}, dimensions={0} | all-to-all | bytes 4194304 | tf_op jit(solution)/shard_map/all_to_all | solution.py:329
  52.6 4.2 %collective-permute-done.other = bf16[16,4,128,128]{3,2,1,0:T(8,128)(2,1)S(1)} collective-permute-done((bf16[16,4,128,128]{3,2,1,0:T(8,128)(2,1)S(1)}, bf16[16,4,128,128]{3,2,1,0:T(8,128)(2,1)S(1)}, u32[]{:S(2)}, u32[]{:S(2)}) %collective-permute-start) | collective-permute-done | bytes 2097184 | tf_op jit(solution)/shard_map/ppermute | solution.py:330
  58.0 15.3 %fit.1 = bf16[16,9,16,1024]{3,2,1,0:T(8,128)(2,1)} custom-call(s32[260]{0:T(512)} %get-tuple-element.31.table, bf16[16,4,128,128]{3,2,1,0:T(8,128)(2,1)} %copy-done, bf16[16,4,128,128]{3,2,1,0:T(8,128)(2,1)} %copy-done.1, bf16[16,5,9,128,128]{4,3,2,1,0:T(8,128)(2,1)} %rest_9_.1, bf16[16,5,9,128,128]{4,3,2,1,0:T(8,128)(2,1)} %rest_9_.1, ...), custom_call_target="tpu_custom_call" | custom-call | tf_op jit(solution)/shard_map/fit/pallas_call | solution.py:128
  73.3 62.4 %all_to_all.17.fitted = bf16[16,9,16,1024]{3,2,1,0:T(8,128)(2,1)} all-to-all(bf16[16,9,16,1024]{3,2,1,0:T(8,128)(2,1)} %fit.1), channel_id=1, replica_groups=mesh['pair'=8,'ri'=16] {'ri'}, dimensions={0} | all-to-all | bytes 9437184 | tf_op jit(solution)/shard_map/all_to_all | solution.py:333
  135.7 17.7 %exchange_panels.1 = (bf16[4,64,1152]{2,1,0:T(8,128)(2,1)}, bf16[4,64,1152]{2,1,0:T(8,128)(2,1)}, bf16[4,64,1152]{2,1,0:T(8,128)(2,1)}, bf16[4,64,1152]{2,1,0:T(...) custom-call(s32[260]{0:T(512)} %get-tuple-element.31.table, ...), custom_call_target="tpu_custom_call" | custom-call | tf_op jit(solution)/shard_map/exchange_panels/pallas_call | solution.py:216
  155.0 1.8 collective-permute-start.3
  157.7 1.8 collective-permute-start.5
  159.5 22.6 %collective-permute-done.1.rest_1_ = bf16[4,64,1152]{2,1,0:T(8,128)(2,1)S(1)} collective-permute-done((bf16[4,64,1152]{2,1,0:T(8,128)(2,1)}, bf16[4,64,1152]{2,1,0:T(8,128)(2,1)S(1)}, u32[]{:S(2)}, u32[]{:S(2)}) %collective-permute-start.1) | collective-permute-done | bytes 589856 | tf_op jit(solution)/shard_map/ppermute | solution.py:338
  182.9 2.0 collective-permute-done.4.rest_5_
  185.0 7.2 %collective-permute-done.6.rest_7_ = bf16[4,64,1152]{2,1,0:T(8,128)(2,1)S(1)} collective-permute-done((bf16[4,64,1152]{2,1,0:T(8,128)(2,1)}, bf16[4,64,1152]{2,1,0:T(8,128)(2,1)S(1)}, u32[]{:S(2)}, u32[]{:S(2)}) %collective-permute-start.6) | collective-permute-done | bytes 589856 | tf_op jit(solution)/shard_map/ppermute | solution.py:339
  193.0 3.8 %first_sum.1 = (f32[64,1152]{1,0:T(8,128)}, bf16[64,1152]{1,0:T(8,128)(2,1)}, bf16[64,1152]{1,0:T(8,128)(2,1)}, bf16[64,1152]{1,0:T(8,128)(2,1)}, f32[64,1152]{1...) custom-call(s32[260]{0:T(512)} %get-tuple-element.31.table, ...), custom_call_target="tpu_custom_call" | custom-call | tf_op jit(solution)/shard_map/first_sum/pallas_call | solution.py:245
  196.9 3.5 %collective-permute-start.8 = (bf16[64,1152]{1,0:T(8,128)(2,1)}, bf16[64,1152]{1,0:T(8,128)(2,1)S(1)}, u32[]{:S(2)}, u32[]{:S(2)}) collective-permute-start(bf16[64,1152]{1,0:T(8,128)(2,1)} %get-tuple-element.43), channel_id=1, source_target_pairs={{0,8},{1,9},{2,10},{3,11},{4,12},{5,13},{6,14},{7,15},{8,0},{9,1},... | collective-permute-start | bytes 442376 | tf_op jit(solution)/shard_map/ppermute | solution.py:338
  201.5 1.9 collective-permute-done.7.refs_1_
  203.6 1.6 collective-permute-done.8.refs_2_
  205.9 2.9 %collective-permute-done.10.refs_5_ = bf16[64,1152]{1,0:T(8,128)(2,1)S(1)} collective-permute-done((bf16[64,1152]{1,0:T(8,128)(2,1)}, bf16[64,1152]{1,0:T(8,128)(2,1)S(1)}, u32[]{:S(2)}, u32[]{:S(2)}) %collective-permute-start.10) | collective-permute-done | bytes 147488 | tf_op jit(solution)/shard_map/ppermute | solution.py:339
  210.4 2.4 %second_sum.1 = (f32[128,1152]{1,0:T(8,128)}, bf16[128,128]{1,0:T(8,128)(2,1)}, bf16[128,128]{1,0:T(8,128)(2,1)}, bf16[128,128]{1,0:T(8,128)(2,1)}, bf16[128,128...) custom-call(f32[64,1152]{1,0:T(8,128)} %get-tuple-element.41.refs_0_, ...), custom_call_target="tpu_custom_call" | custom-call | tf_op jit(solution)/shard_map/second_sum/pallas_call | solution.py:275
  212.9 3.8 %collective-permute-start.14 = (bf16[128,128]{1,0:T(8,128)(2,1)}, bf16[128,128]{1,0:T(8,128)(2,1)S(1)}, u32[]{:S(2)}, u32[]{:S(2)}) collective-permute-start(bf16[128,128]{1,0:T(8,128)(2,1)} %get-tuple-element.51), channel_id=1, source_target_pairs={{0,2},{1,3},{2,4},{3,5},{4,6},{5,7},{6,8},{7,9},{8,10},{9,11},{10,... | collective-permute-start | bytes 98312 | tf_op jit(solution)/shard_map/ppermute | solution.py:345
  219.1 1.5 collective-permute-start.17
  220.6 3.0 %collective-permute-start.18 = (bf16[128,128]{1,0:T(8,128)(2,1)}, bf16[128,128]{1,0:T(8,128)(2,1)S(1)}, u32[]{:S(2)}, u32[]{:S(2)}) collective-permute-start(bf16[128,128]{1,0:T(8,128)(2,1)} %get-tuple-element.55), channel_id=1, source_target_pairs={{0,6},{1,7},{2,8},{3,9},{4,10},{5,11},{6,12},{7,13},{8,14},{9,15},... | collective-permute-start | bytes 98312 | tf_op jit(solution)/shard_map/ppermute | solution.py:345
  223.6 2.7 %collective-permute-start.19 = (bf16[128,128]{1,0:T(8,128)(2,1)}, bf16[128,128]{1,0:T(8,128)(2,1)S(1)}, u32[]{:S(2)}, u32[]{:S(2)}) collective-permute-start(bf16[128,128]{1,0:T(8,128)(2,1)} %get-tuple-element.56), channel_id=1, source_target_pairs={{0,7},{1,8},{2,9},{3,10},{4,11},{5,12},{6,13},{7,14},{8,15},{9,0},... | collective-permute-start | bytes 98312 | tf_op jit(solution)/shard_map/ppermute | solution.py:345
  226.8 1.8 collective-permute-done.18.rest_5_
  230.8 2.2 place_blocks.1
  (71 shorter events, 17.9 us)
Async XLA Ops:
  52.6 4.2 %collective-permute-start = (bf16[16,4,128,128]{3,2,1,0:T(8,128)(2,1)S(1)}, bf16[16,4,128,128]{3,2,1,0:T(8,128)(2,1)S(1)}, u32[]{:S(2)}, u32[]{:S(2)}) collective-permute-start(bf16[16,4,128,128]{3,2,1,0:T(8,128)(2,1)S(1)} %all_to_all.16.same), channel_id=1, source_target_pairs={{0,16},{16,0},{32,48},{48,32},{64,80},{80,64},{96,112},{112,96},{1... | collective-permute-start | bytes 6291464 | tf_op jit(solution)/shard_map/ppermute | solution.py:330
  153.4 28.7 %collective-permute-start.1 = (bf16[4,64,1152]{2,1,0:T(8,128)(2,1)}, bf16[4,64,1152]{2,1,0:T(8,128)(2,1)S(1)}, u32[]{:S(2)}, u32[]{:S(2)}) collective-permute-start(bf16[4,64,1152]{2,1,0:T(8,128)(2,1)} %get-tuple-element.34), channel_id=1, source_target_pairs={{0,1},{1,2},{2,3},{3,0},{4,5},{5,6},{6,7},{7,4},{8,9},{9,10},{10,1... | collective-permute-start | bytes 1769480 | tf_op jit(solution)/shard_map/ppermute | solution.py:338
  153.9 29.0 %collective-permute-start.2 = (bf16[4,64,1152]{2,1,0:T(8,128)(2,1)}, bf16[4,64,1152]{2,1,0:T(8,128)(2,1)S(1)}, u32[]{:S(2)}, u32[]{:S(2)}) collective-permute-start(bf16[4,64,1152]{2,1,0:T(8,128)(2,1)} %get-tuple-element.35), channel_id=1, source_target_pairs={{0,2},{1,3},{2,0},{3,1},{4,6},{5,7},{6,4},{7,5},{8,10},{9,11},{10,... | collective-permute-start | bytes 1769480 | tf_op jit(solution)/shard_map/ppermute | solution.py:338
  155.0 28.0 %collective-permute-start.3 = (bf16[4,64,1152]{2,1,0:T(8,128)(2,1)}, bf16[4,64,1152]{2,1,0:T(8,128)(2,1)S(1)}, u32[]{:S(2)}, u32[]{:S(2)}) collective-permute-start(bf16[4,64,1152]{2,1,0:T(8,128)(2,1)} %get-tuple-element.36), channel_id=1, source_target_pairs={{0,3},{1,0},{2,1},{3,2},{4,7},{5,4},{6,5},{7,6},{8,11},{9,8},{10,9... | collective-permute-start | bytes 1769480 | tf_op jit(solution)/shard_map/ppermute | solution.py:338
  156.8 28.2 %collective-permute-start.4 = (bf16[4,64,1152]{2,1,0:T(8,128)(2,1)}, bf16[4,64,1152]{2,1,0:T(8,128)(2,1)S(1)}, u32[]{:S(2)}, u32[]{:S(2)}) collective-permute-start(bf16[4,64,1152]{2,1,0:T(8,128)(2,1)} %get-tuple-element.38), channel_id=1, source_target_pairs={{0,4},{1,5},{2,6},{3,7},{4,8},{5,9},{6,10},{7,11},{8,12},{9,13},{1... | collective-permute-start | bytes 1769480 | tf_op jit(solution)/shard_map/ppermute | solution.py:339
  157.7 27.3 %collective-permute-start.5 = (bf16[4,64,1152]{2,1,0:T(8,128)(2,1)}, bf16[4,64,1152]{2,1,0:T(8,128)(2,1)S(1)}, u32[]{:S(2)}, u32[]{:S(2)}) collective-permute-start(bf16[4,64,1152]{2,1,0:T(8,128)(2,1)} %get-tuple-element.39), channel_id=1, source_target_pairs={{0,8},{1,9},{2,10},{3,11},{4,12},{5,13},{6,14},{7,15},{8,0},{9,1},... | collective-permute-start | bytes 1769480 | tf_op jit(solution)/shard_map/ppermute | solution.py:339
  182.1 10.1 %copy-start.2 = (bf16[4,64,1152]{2,1,0:T(8,128)(2,1)}, bf16[4,64,1152]{2,1,0:T(8,128)(2,1)S(1)}, u32[]{:S(2)}) copy-start(bf16[4,64,1152]{2,1,0:T(8,128)(2,1)S(1)} %collective-permute-done.1.rest_1_) | copy-start | bytes 1769476
  182.1 10.1 %collective-permute-start.6 = (bf16[4,64,1152]{2,1,0:T(8,128)(2,1)}, bf16[4,64,1152]{2,1,0:T(8,128)(2,1)S(1)}, u32[]{:S(2)}, u32[]{:S(2)}) collective-permute-start(bf16[4,64,1152]{2,1,0:T(8,128)(2,1)} %get-tuple-element.40), channel_id=1, source_target_pairs={{0,12},{1,13},{2,14},{3,15},{4,0},{5,1},{6,2},{7,3},{8,4},{9,5},{1... | collective-permute-start | bytes 1769480 | tf_op jit(solution)/shard_map/ppermute | solution.py:339
  182.9 9.3 %copy-start.3 = (bf16[4,64,1152]{2,1,0:T(8,128)(2,1)}, bf16[4,64,1152]{2,1,0:T(8,128)(2,1)S(1)}, u32[]{:S(2)}) copy-start(bf16[4,64,1152]{2,1,0:T(8,128)(2,1)S(1)} %collective-permute-done.2.rest_2_) | copy-start | bytes 1769476
  182.9 9.3 %copy-start.4 = (bf16[4,64,1152]{2,1,0:T(8,128)(2,1)}, bf16[4,64,1152]{2,1,0:T(8,128)(2,1)S(1)}, u32[]{:S(2)}) copy-start(bf16[4,64,1152]{2,1,0:T(8,128)(2,1)S(1)} %collective-permute-done.3.rest_3_) | copy-start | bytes 1769476
  196.9 6.6 %collective-permute-start.7 = (bf16[64,1152]{1,0:T(8,128)(2,1)}, bf16[64,1152]{1,0:T(8,128)(2,1)S(1)}, u32[]{:S(2)}, u32[]{:S(2)}) collective-permute-start(bf16[64,1152]{1,0:T(8,128)(2,1)} %get-tuple-element.42), channel_id=1, source_target_pairs={{0,4},{1,5},{2,6},{3,7},{4,8},{5,9},{6,10},{7,11},{8,12},{9,13},{1... | collective-permute-start | bytes 442376 | tf_op jit(solution)/shard_map/ppermute | solution.py:338
  196.9 8.4 %collective-permute-start.8 = (bf16[64,1152]{1,0:T(8,128)(2,1)}, bf16[64,1152]{1,0:T(8,128)(2,1)S(1)}, u32[]{:S(2)}, u32[]{:S(2)}) collective-permute-start(bf16[64,1152]{1,0:T(8,128)(2,1)} %get-tuple-element.43), channel_id=1, source_target_pairs={{0,8},{1,9},{2,10},{3,11},{4,12},{5,13},{6,14},{7,15},{8,0},{9,1},... | collective-permute-start | bytes 442376 | tf_op jit(solution)/shard_map/ppermute | solution.py:338
  200.3 5.6 %collective-permute-start.9 = (bf16[64,1152]{1,0:T(8,128)(2,1)}, bf16[64,1152]{1,0:T(8,128)(2,1)S(1)}, u32[]{:S(2)}, u32[]{:S(2)}) collective-permute-start(bf16[64,1152]{1,0:T(8,128)(2,1)} %get-tuple-element.44), channel_id=1, source_target_pairs={{0,12},{1,13},{2,14},{3,15},{4,0},{5,1},{6,2},{7,3},{8,4},{9,5},{1... | collective-permute-start | bytes 442376 | tf_op jit(solution)/shard_map/ppermute | solution.py:338
  200.3 8.5 %collective-permute-start.10 = (bf16[64,1152]{1,0:T(8,128)(2,1)}, bf16[64,1152]{1,0:T(8,128)(2,1)S(1)}, u32[]{:S(2)}, u32[]{:S(2)}) collective-permute-start(bf16[64,1152]{1,0:T(8,128)(2,1)} %get-tuple-element.46), channel_id=1, source_target_pairs={{0,1},{1,2},{2,3},{3,0},{4,5},{5,6},{6,7},{7,4},{8,9},{9,10},{10,1... | collective-permute-start | bytes 442376 | tf_op jit(solution)/shard_map/ppermute | solution.py:339
  200.3 8.5 %collective-permute-start.11 = (bf16[64,1152]{1,0:T(8,128)(2,1)}, bf16[64,1152]{1,0:T(8,128)(2,1)S(1)}, u32[]{:S(2)}, u32[]{:S(2)}) collective-permute-start(bf16[64,1152]{1,0:T(8,128)(2,1)} %get-tuple-element.47), channel_id=1, source_target_pairs={{0,2},{1,3},{2,0},{3,1},{4,6},{5,7},{6,4},{7,5},{8,10},{9,11},{10,... | collective-permute-start | bytes 442376 | tf_op jit(solution)/shard_map/ppermute | solution.py:339
  203.4 6.3 %collective-permute-start.12 = (bf16[64,1152]{1,0:T(8,128)(2,1)}, bf16[64,1152]{1,0:T(8,128)(2,1)S(1)}, u32[]{:S(2)}, u32[]{:S(2)}) collective-permute-start(bf16[64,1152]{1,0:T(8,128)(2,1)} %get-tuple-element.48), channel_id=1, source_target_pairs={{0,3},{1,0},{2,1},{3,2},{4,7},{5,4},{6,5},{7,6},{8,11},{9,8},{10,9... | collective-permute-start | bytes 442376 | tf_op jit(solution)/shard_map/ppermute | solution.py:339
  212.8 7.8 %collective-permute-start.13 = (bf16[128,128]{1,0:T(8,128)(2,1)}, bf16[128,128]{1,0:T(8,128)(2,1)S(1)}, u32[]{:S(2)}, u32[]{:S(2)}) collective-permute-start(bf16[128,128]{1,0:T(8,128)(2,1)} %get-tuple-element.50), channel_id=1, source_target_pairs={{0,1},{1,2},{2,3},{3,4},{4,5},{5,6},{6,7},{7,8},{8,9},{9,10},{10,1... | collective-permute-start | bytes 98312 | tf_op jit(solution)/shard_map/ppermute | solution.py:345
  212.9 10.7 %collective-permute-start.14 = (bf16[128,128]{1,0:T(8,128)(2,1)}, bf16[128,128]{1,0:T(8,128)(2,1)S(1)}, u32[]{:S(2)}, u32[]{:S(2)}) collective-permute-start(bf16[128,128]{1,0:T(8,128)(2,1)} %get-tuple-element.51), channel_id=1, source_target_pairs={{0,2},{1,3},{2,4},{3,5},{4,6},{5,7},{6,8},{7,9},{8,10},{9,11},{10,... | collective-permute-start | bytes 98312 | tf_op jit(solution)/shard_map/ppermute | solution.py:345
  216.7 9.6 %collective-permute-start.15 = (bf16[128,128]{1,0:T(8,128)(2,1)}, bf16[128,128]{1,0:T(8,128)(2,1)S(1)}, u32[]{:S(2)}, u32[]{:S(2)}) collective-permute-start(bf16[128,128]{1,0:T(8,128)(2,1)} %get-tuple-element.52), channel_id=1, source_target_pairs={{0,3},{1,4},{2,5},{3,6},{4,7},{5,8},{6,9},{7,10},{8,11},{9,12},{10... | collective-permute-start | bytes 98312 | tf_op jit(solution)/shard_map/ppermute | solution.py:345
  217.9 8.4 %collective-permute-start.16 = (bf16[128,128]{1,0:T(8,128)(2,1)}, bf16[128,128]{1,0:T(8,128)(2,1)S(1)}, u32[]{:S(2)}, u32[]{:S(2)}) collective-permute-start(bf16[128,128]{1,0:T(8,128)(2,1)} %get-tuple-element.53), channel_id=1, source_target_pairs={{0,4},{1,5},{2,6},{3,7},{4,8},{5,9},{6,10},{7,11},{8,12},{9,13},{1... | collective-permute-start | bytes 98312 | tf_op jit(solution)/shard_map/ppermute | solution.py:345
  219.1 7.7 %collective-permute-start.17 = (bf16[128,128]{1,0:T(8,128)(2,1)}, bf16[128,128]{1,0:T(8,128)(2,1)S(1)}, u32[]{:S(2)}, u32[]{:S(2)}) collective-permute-start(bf16[128,128]{1,0:T(8,128)(2,1)} %get-tuple-element.54), channel_id=1, source_target_pairs={{0,5},{1,6},{2,7},{3,8},{4,9},{5,10},{6,11},{7,12},{8,13},{9,14},{... | collective-permute-start | bytes 98312 | tf_op jit(solution)/shard_map/ppermute | solution.py:345
  220.6 9.5 %copy-start.14 = (bf16[128,128]{1,0:T(8,128)(2,1)}, bf16[128,128]{1,0:T(8,128)(2,1)S(1)}, u32[]{:S(2)}) copy-start(bf16[128,128]{1,0:T(8,128)(2,1)S(1)} %collective-permute-done.13.rest_0_) | copy-start | bytes 98308
  220.6 8.0 %collective-permute-start.18 = (bf16[128,128]{1,0:T(8,128)(2,1)}, bf16[128,128]{1,0:T(8,128)(2,1)S(1)}, u32[]{:S(2)}, u32[]{:S(2)}) collective-permute-start(bf16[128,128]{1,0:T(8,128)(2,1)} %get-tuple-element.55), channel_id=1, source_target_pairs={{0,6},{1,7},{2,8},{3,9},{4,10},{5,11},{6,12},{7,13},{8,14},{9,15},... | collective-permute-start | bytes 98312 | tf_op jit(solution)/shard_map/ppermute | solution.py:345
  223.6 6.5 %collective-permute-start.19 = (bf16[128,128]{1,0:T(8,128)(2,1)}, bf16[128,128]{1,0:T(8,128)(2,1)S(1)}, u32[]{:S(2)}, u32[]{:S(2)}) collective-permute-start(bf16[128,128]{1,0:T(8,128)(2,1)} %get-tuple-element.56), channel_id=1, source_target_pairs={{0,7},{1,8},{2,9},{3,10},{4,11},{5,12},{6,13},{7,14},{8,15},{9,0},... | collective-permute-start | bytes 98312 | tf_op jit(solution)/shard_map/ppermute | solution.py:345
  (17 other events, 57.6 us)

commit v3 on v2

v3 whole, which is shorter than its diff:
```python
import functools

import jax
import jax.numpy as jnp
from jax import lax
from jax.experimental import pallas as pl
from jax.experimental.pallas import tpu as pltpu
from jax.sharding import PartitionSpec as P

MIB = 1024 * 1024
NT = (((1,), (1,)), ((), ()))
SIDE = 4
HALVES = 2
CHUNKS = 2
ON_VMEM = pl.BlockSpec(memory_space=pltpu.VMEM)
ON_SMEM = pl.BlockSpec(memory_space=pltpu.SMEM)


class Table:
    def __init__(self, blocks, slots):
        self.blocks, self.slots = blocks, slots
        self.count = 0
        self.slot = self.count + blocks
        self.core = self.slot + blocks * slots
        self.top = self.core + blocks * slots
        self.low = self.top + blocks * slots
        self.ri = self.low + blocks * slots
        self.x, self.y = self.ri + 1, self.ri + 2
        self.size = self.ri + 3


def prepare_kernel(at, place, lam, tile_count, screen, table):
    ri, x, y, z, core = (place[n] for n in range(5))
    for n in range(3):
        table[at.ri + n] = place[n]

    def one(b, _):
        count = jnp.int32(0)
        for s in range(at.slots):
            keep = jnp.logical_and(s < tile_count[b], screen[b, s] > 0)
            to = b * at.slots + count
            name = lam[b, s]

            part, place_ri = lax.div(name, SIDE * SIDE), lax.rem(name, SIDE * SIDE)
            back_x = lax.rem(x + SIDE - lax.rem(place_ri, SIDE), SIDE)
            back_y = lax.rem(y + SIDE - lax.div(place_ri, SIDE), SIDE)
            back_z = lax.rem(z + SIDE - lax.div(part, 2), SIDE)

            @pl.when(keep)
            def _():
                table[at.slot + to] = s
                table[at.core + to] = lax.rem(part + core, 2)
                table[at.top + to] = (back_y * SIDE + back_x) * SIDE + back_z
                table[at.low + to] = (back_x * SIDE + back_y) * SIDE + back_z

            count = count + keep.astype(jnp.int32)
        table[at.count + b] = count
        return 0

    lax.fori_loop(0, at.blocks, one, 0)


def prepare(at, place, lam, tile_count, screen):
    return pl.pallas_call(
        functools.partial(prepare_kernel, at),
        in_specs=[ON_SMEM] * 4,
        out_specs=ON_SMEM,
        out_shape=jax.ShapeDtypeStruct((at.size,), jnp.int32),
        name="prepare",
    )(place, lam, tile_count, screen)


def gather(coefficients):
    pairs = lax.axis_size("pair")
    half = coefficients.shape[0] // 2

    def around(value, axis, shift):
        return jnp.stack([value] + [lax.ppermute(value, axis, shift(k)) for k in range(1, SIDE)])

    column = around(coefficients, "pair", lambda k: [(p, (p + 2 * k) % pairs) for p in range(pairs)])
    top = around(around(column[:, :half], "ri", along_x), "ri", along_y)
    low = around(around(column[:, half:], "ri", along_y), "ri", along_x)
    same = jnp.stack([top, low]).reshape((2, SIDE ** 3) + top.shape[3:])
    return same, lax.ppermute(same, "pair", [(p, p ^ 1) for p in range(pairs)])


def fit_kernel(at, table, same, other, integrals, out, tiles, picked, total, done):
    slots = at.slots
    _, _, cut, size = same.shape
    ri, own_q, rows, _ = out.shape
    share = rows // HALVES
    steps = at.blocks // HALVES

    def copy(block, j):
        slot = table[at.slot + block * slots + j]
        return pltpu.make_async_copy(integrals.at[block, slot], tiles.at[block, j], done.at[block, j])

    def kept(block, act):
        for j in range(slots):
            @pl.when(j < table[at.count + block])
            def _():
                act(copy(block, j))

    def begin(step, _):
        for half in range(HALVES):
            kept(step + half * steps, lambda c: c.start())
        return 0

    lax.fori_loop(0, steps, begin, 0)

    def one(step, _):
        for half in range(HALVES):
            block = step + half * steps
            count = table[at.count + block]
            kept(block, lambda c: c.wait())

            @pl.when(count == 0)
            def _():
                total[half] = jnp.zeros(total.shape[1:], total.dtype)

            for c in range(1, slots + 1):
                @pl.when(count == c)
                def _():
                    for j in range(c):
                        n = block * slots + j
                        for part, start in enumerate((at.top, at.low)):
                            name = table[start + n]
                            tile = jnp.where(table[at.core + n] == 0, same[part, name], other[part, name])
                            picked[half, part * cut:(part + 1) * cut, j * size:(j + 1) * size] = tile
                    wide = [tiles[block, j].reshape(own_q * size, size) for j in range(c)]
                    wide = jnp.concatenate(wide, axis=1) if c > 1 else wide[0]
                    total[half] = lax.dot_general(
                        picked[half, :, :c * size], wide, NT, preferred_element_type=jnp.float32
                    )

        for q in range(own_q):
            parts = [
                total[half, :, q * size:(q + 1) * size].reshape(ri, share, size) for half in range(HALVES)
            ]
            out[:, q, :, pl.ds(pl.multiple_of(step * size, size), size)] = (
                jnp.concatenate(parts, axis=1).astype(out.dtype)
            )
        return 0

    lax.fori_loop(0, steps, one, 0)


def fit(at, table, integrals, same, other):
    blocks, slots, own_q, size, _ = integrals.shape
    occupied = 2 * same.shape[2]
    ri = SIDE * SIDE
    share = occupied // ri
    return pl.pallas_call(
        functools.partial(fit_kernel, at),
        in_specs=[ON_SMEM, ON_VMEM, ON_VMEM, pl.BlockSpec(memory_space=pl.ANY)],
        out_specs=ON_VMEM,
        scratch_shapes=[
            pltpu.VMEM((blocks, slots, own_q, size, size), jnp.bfloat16),
            pltpu.VMEM((HALVES, occupied, slots * size), jnp.bfloat16),
            pltpu.VMEM((HALVES, occupied, own_q * size), jnp.float32),
            pltpu.SemaphoreType.DMA((blocks, slots)),
        ],
        out_shape=jax.ShapeDtypeStruct((ri, own_q, HALVES * share, blocks // HALVES * size), jnp.bfloat16),
        compiler_params=pltpu.CompilerParams(vmem_limit_bytes=40 * MIB),
        cost_estimate=pl.CostEstimate(flops=3 * 10 ** 9, bytes_accessed=20 * 10 ** 6, transcendentals=0),
        name="fit",
    )(table, same, other, integrals)


def factor_kernel(metric, fitted, factors, turned, wide):
    ri, own_q, rows, half_cols = fitted.shape
    share = rows // HALVES
    n_q = metric.shape[0]
    lanes, tile = wide.shape[1], wide.shape[3]
    chunk = lanes * tile

    def one(c, _):
        base = pl.multiple_of(c * chunk, chunk)
        for k in range(own_q):
            x = fitted[:, k, :, pl.ds(base, chunk)].astype(jnp.float32)
            for r in range(ri):
                to = (r * own_q + k) * share
                for h in range(HALVES):
                    for t in range(lanes):
                        wide[h, t, to:to + share, :] = x[r, h * share:(h + 1) * share, t * tile:(t + 1) * tile]
        for h in range(HALVES):
            start = pl.multiple_of(base + h * half_cols, chunk)
            parts = []
            for o in range(share):
                x = jnp.concatenate(
                    [wide[h, t, pl.ds(o, n_q, stride=share), :] for t in range(lanes)], axis=1
                ).astype(jnp.bfloat16)
                parts.append(jnp.dot(metric[...], x, preferred_element_type=jnp.float32).astype(jnp.bfloat16))
            whole = jnp.concatenate(parts, axis=0)
            factors[:, pl.ds(start, chunk)] = whole
            if h == 0:
                factors[:, pl.ds(pl.multiple_of(base + HALVES * half_cols, chunk), chunk)] = whole
            turned[pl.ds(start, chunk), :] = whole.T
        return 0

    lax.fori_loop(0, half_cols // chunk, one, 0)


def factor(metric, fitted):
    ri, own_q, rows, half_cols = fitted.shape
    cols = HALVES * half_cols
    depth = own_q * ri * rows // HALVES
    return pl.pallas_call(
        factor_kernel,
        in_specs=[ON_VMEM] * 2,
        out_specs=[ON_VMEM] * 2,
        out_shape=[
            jax.ShapeDtypeStruct((depth, cols + half_cols), jnp.bfloat16),
            jax.ShapeDtypeStruct((cols, depth), jnp.bfloat16),
        ],
        scratch_shapes=[pltpu.VMEM((HALVES, 2, depth, cols // ri), jnp.float32)],
        compiler_params=pltpu.CompilerParams(vmem_limit_bytes=28 * MIB),
        cost_estimate=pl.CostEstimate(flops=2 * 10 ** 9, bytes_accessed=10 * 10 ** 6, transcendentals=0),
        name="factor",
    )(metric, fitted)


def panel_kernel(at, first, table, factors, turned, *rest):
    by_x, by_y, panels = rest[:SIDE], rest[SIDE:2 * SIDE], rest[2 * SIDE]
    ri, size, span = panels.shape
    cut = size // 2

    def two(n, _):
        start = pl.multiple_of(n * 2 * size, 2 * size)
        value = jnp.dot(
            turned[pl.ds(start, 2 * size), :],
            factors[:, pl.ds(start + first * size, span + size)],
            preferred_element_type=jnp.float32,
        ).astype(jnp.bfloat16)
        for side in range(2):
            panels[2 * n + side] = value[side * size:(side + 1) * size, side * size:side * size + span]
        return 0

    lax.fori_loop(0, ri // 2, two, 0)
    for k in range(SIDE):
        x = lax.rem(table[at.x] + k, SIDE)
        y = lax.rem(table[at.y] + k, SIDE)
        for j in range(SIDE):
            by_x[k][j] = panels[j * SIDE + x, :cut]
            by_y[k][j] = panels[y * SIDE + j, cut:]


def panel_columns(at, first, last, table, factors, turned):
    cols, depth = turned.shape
    size = cols // (SIDE * SIDE)
    span = (last - first) * size
    return pl.pallas_call(
        functools.partial(panel_kernel, at, first),
        in_specs=[ON_SMEM, ON_VMEM, ON_VMEM],
        out_specs=[ON_VMEM] * (2 * SIDE),
        out_shape=[jax.ShapeDtypeStruct((SIDE, size // 2, span), jnp.bfloat16)] * (2 * SIDE),
        scratch_shapes=[pltpu.VMEM((SIDE * SIDE, size, span), jnp.bfloat16)],
        compiler_params=pltpu.CompilerParams(vmem_limit_bytes=24 * MIB),
        cost_estimate=pl.CostEstimate(
            flops=8 * 10 ** 8 * (last - first), bytes_accessed=15 * 10 ** 6, transcendentals=0
        ),
        name="panel_columns",
    )(table, factors, turned)


def first_sum_kernel(at, table, *rest):
    ins, outs = rest[:2 * SIDE], rest[2 * SIDE:]
    for path, mine in enumerate((table[at.y], table[at.x])):
        for k in range(SIDE):
            to = lax.rem(mine + k, SIDE)
            total = ins[path * SIDE][to].astype(jnp.float32)
            for j in range(1, SIDE):
                total = total + ins[path * SIDE + j][to].astype(jnp.float32)
            out = outs[path * SIDE + k]
            out[...] = total.astype(out.dtype)


def first_sum(at, table, parts):
    shape = parts[0].shape[1:]
    return pl.pallas_call(
        functools.partial(first_sum_kernel, at),
        in_specs=[ON_SMEM] + [ON_VMEM] * len(parts),
        out_specs=[ON_VMEM] * len(parts),
        out_shape=[
            jax.ShapeDtypeStruct(shape, jnp.float32 if n % SIDE == 0 else jnp.bfloat16)
            for n in range(len(parts))
        ],
        compiler_params=pltpu.CompilerParams(vmem_limit_bytes=16 * MIB),
        name="first_sum",
    )(table, *parts)


def second_sum_kernel(skip, *refs):
    ins, own, mirrors = refs[:2 * SIDE], refs[2 * SIDE], refs[2 * SIDE + 1:]
    cut = ins[0].shape[0]
    size = 2 * cut
    for path in range(2):
        total = ins[path * SIDE][...]
        for j in range(1, SIDE):
            total = total + ins[path * SIDE + j][...].astype(jnp.float32)
        own[path * cut:(path + 1) * cut, :] = total
    for d, mirror in enumerate(mirrors, skip):
        mirror[...] = own[:, d * size:(d + 1) * size].T.astype(mirror.dtype)


def second_sum(skip, mirrors, parts):
    cut, span = parts[0].shape
    size = 2 * cut
    return pl.pallas_call(
        functools.partial(second_sum_kernel, skip),
        in_specs=[ON_VMEM] * len(parts),
        out_specs=[ON_VMEM] * (1 + mirrors),
        out_shape=[jax.ShapeDtypeStruct((size, span), jnp.float32)]
        + [jax.ShapeDtypeStruct((size, size), jnp.bfloat16)] * mirrors,
        compiler_params=pltpu.CompilerParams(vmem_limit_bytes=16 * MIB),
        name="second_sum",
    )(*parts)


def place_kernel(at, table, *rest):
    owns, mirrors, out = rest[:CHUNKS], rest[CHUNKS:-1], rest[-1]
    size = out.shape[0]
    ri = out.shape[1] // size
    d = 0
    for own in owns:
        for n in range(own.shape[1] // size):
            to = lax.rem(table[at.ri] + d, ri) * size
            out[:, pl.ds(pl.multiple_of(to, size), size)] = own[:, n * size:(n + 1) * size]
            d += 1
    for d, mirror in enumerate(mirrors, 1):
        to = lax.rem(table[at.ri] + ri - d, ri) * size
        out[:, pl.ds(pl.multiple_of(to, size), size)] = mirror[...].astype(out.dtype)


def place_blocks(at, table, owns, mirrors):
    size = owns[0].shape[0]
    ri = len(mirrors) * 2 + 2
    return pl.pallas_call(
        functools.partial(place_kernel, at),
        in_specs=[ON_SMEM] + [ON_VMEM] * (CHUNKS + len(mirrors)),
        out_specs=ON_VMEM,
        out_shape=jax.ShapeDtypeStruct((size, ri * size), jnp.float32),
        name="place_blocks",
    )(table, *owns, *mirrors)


def along_x(k):
    return [(y * SIDE + x, y * SIDE + (x + k) % SIDE) for y in range(SIDE) for x in range(SIDE)]


def along_y(k):
    return [(y * SIDE + x, (y + k) % SIDE * SIDE + x) for y in range(SIDE) for x in range(SIDE)]


def body(integrals, lam_index, tile_count, screen, coefficients, metric):
    ri = lax.axis_size("ri")
    at = Table(*integrals.shape[:2])
    here = lax.axis_index("ri").astype(jnp.int32)
    part = lax.axis_index("pair").astype(jnp.int32)
    place = jnp.stack([here, lax.rem(here, SIDE), lax.div(here, SIDE), lax.div(part, 2), lax.rem(part, 2)])
    table = prepare(at, place, lam_index, tile_count, screen)
    same, other = gather(coefficients)
    mine = fit(at, table, integrals, same, other)
    fitted = lax.all_to_all(mine, "ri", 0, 0, tiled=True)
    factors, turned = factor(metric, fitted)

    def exchange_two(parts, first, second):
        return (
            parts[:1] + [lax.ppermute(parts[k], "ri", first(k)) for k in range(1, SIDE)]
            + parts[SIDE:SIDE + 1] + [lax.ppermute(parts[SIDE + k], "ri", second(k)) for k in range(1, SIDE)]
        )

    cuts = (0, ri // 4 + 1, ri // 2 + 1)
    owns, mirrors = [], []
    for first, last in zip(cuts, cuts[1:]):
        skip = 1 if first == 0 else 0
        count = min(last, ri // 2) - first - skip
        panels = panel_columns(at, first, last, table, factors, turned)
        sums = first_sum(at, table, exchange_two(list(panels), along_x, along_y))
        own, *turned_blocks = second_sum(skip, count, exchange_two(list(sums), along_y, along_x))
        owns.append(own)
        for block in turned_blocks:
            d = len(mirrors) + 1
            mirrors.append(lax.ppermute(block, "ri", [(i, (i + d) % ri) for i in range(ri)]))
    return place_blocks(at, table, owns, mirrors)


def solution(mesh):
    placed = (
        P("pair", None, "ri", None, None),
        P("pair", None),
        P("pair"),
        P("pair", None),
        P(None, ("pair", "ri")),
        P(),
    )
    return jax.shard_map(
        body, mesh=mesh, in_specs=placed, out_specs=P(("pair", "ri"), None), check_vma=False
    )
```

time: 238 us -> 216 us (0.908)
  blocking collectives: 109 us -> 64.1 us
  starting transfers between devices: 25.3 us -> 66.7 us
  Pallas kernels: 44 us -> 34.5 us
  waiting for transfers between devices: 47.8 us -> 41.3 us
    all_to_all x2 -> x0, blocking collectives: 46.2 us -> none  [the longest x1 34.8 us: body(): same = lax.all_to_all(column, 'ri', 0, 0, tiled=True)]
    ppermute x8 -> x23, starting transfers between devices: 13.5 us -> 39.4 us  [the longest x15 27.1 us: around(): lax.ppermute(value, axis, shift(k))]
    ppermute x6 -> x12, waiting for transfers between devices: 26.8 us -> 4.85 us  [exchange_two(): lax.ppermute(parts[k], 'ri', first(k))]
    ppermute x8 -> x23, waiting for transfers between devices: 7.98 us -> 20.6 us  [the longest x15 15.8 us: around(): lax.ppermute(value, axis, shift(k))]
    pallas_call x3 -> x6, Pallas kernels: 35.4 us -> 27.2 us  [the longest x2 12.4 us: panel_columns(): pl.pallas_call(functools.partial(panel_kernel, at, first), in_specs=[ON_S...]
    ppermute x6 -> x12, starting transfers between devices: 6.88 us -> 15 us  [exchange_two(): lax.ppermute(parts[k], 'ri', first(k))]
    ppermute x6 -> x12, starting transfers between devices: 4.94 us -> 12.3 us  [exchange_two(): lax.ppermute(parts[SIDE + k], 'ri', second(k))]
    ppermute x6 -> x12, waiting for transfers between devices: 13.1 us -> 15.8 us  [exchange_two(): lax.ppermute(parts[SIDE + k], 'ri', second(k))]
  transfers between devices with their start and end apart: 20 -> 47, of which waited for: 12 -> 21; matrix products, arithmetic and copies ran while one was open for 0% -> 1% of each run, Pallas kernels for 0% -> 5%
where the time goes in v3:
time: 216 us; the launch traced here: 213 us
  starting transfers between devices  66.7 us (31%)
  blocking collectives  64.1 us (30%)
  waiting for transfers between devices  41.3 us (19%)
  Pallas kernels  34.5 us (16%)
  local copies, waits for them, and re-layouts  4.69 us (2%)
    all_to_all x1, blocking collectives, body(): fitted = lax.all_to_all(mine, 'ri', 0, 0, tiled=True)  64.1 us
    ppermute x15, starting transfers between devices, around(): lax.ppermute(value, axis, shift(k))  27.1 us
    ppermute x12, waiting for transfers between devices, exchange_two(): lax.ppermute(parts[SIDE + k], 'ri', second(k))  15.8 us
    ppermute x15, waiting for transfers between devices, around(): lax.ppermute(value, axis, shift(k))  15.8 us
    ppermute x12, starting transfers between devices, exchange_two(): lax.ppermute(parts[k], 'ri', first(k))  15 us
    pallas_call x2, Pallas kernels, panel_columns(): pl.pallas_call(functools.partial(panel_kernel, at, first), in_specs=[ON_S...  12.4 us
    ppermute x12, starting transfers between devices, exchange_two(): lax.ppermute(parts[SIDE + k], 'ri', second(k))  12.3 us
    ppermute x7, starting transfers between devices, body(): lax.ppermute(block, 'ri', [(i, (i + d) % ri) for i in range(ri)])  12.3 us
  transfers between devices with their start and end apart: 47, of which 21 were waited for; matrix products, arithmetic and copies ran while one was open for 1% of the time, Pallas kernels for 5%

profile of v3, /device:TPU:0, one launch (start us, length us, event | category | flops | bytes accessed | tf_op | source)
XLA Modules:
  0.0 212.8 jit_solution(14910778901914539945)
XLA Ops:
  2.0 3.6 %collective-permute-start.1 = (bf16[128,128]{1,0:T(8,128)(2,1)}, bf16[128,128]{1,0:T(8,128)(2,1)S(1)}, u32[]{:S(2)}, u32[]{:S(2)}) collective-permute-start(bf16[128,128]{1,0:T(8,128)(2,1)} %param.10), channel_id=1, source_target_pairs={{0,64},{16,80},{32,96},{48,112},{64,0},{80,16},{96,32},{112,48},{1... | collective-permute-start | bytes 98312 | tf_op jit(solution)/shard_map/ppermute | solution.py:78
  12.1 2.7 %collective-permute-start.4 = (bf16[4,64,128]{2,1,0:T(8,128)(2,1)S(1)}, bf16[4,64,128]{2,1,0:T(8,128)(2,1)S(1)}, u32[]{:S(2)}, u32[]{:S(2)}) collective-permute-start(bf16[4,64,128]{2,1,0:T(8,128)(2,1)S(1)} %get-tuple-element.98), channel_id=1, source_target_pairs={{0,2},{1,3},{2,0},{3,1},{4,6},{5,7},{6,4},{7,5},{8,10},{9,11},{10,... | collective-permute-start | bytes 196616 | tf_op jit(solution)/shard_map/ppermute | solution.py:78
  23.9 2.4 %collective-permute-start.11 = (bf16[4,64,128]{2,1,0:T(8,128)(2,1)S(1)}, bf16[4,64,128]{2,1,0:T(8,128)(2,1)S(1)}, u32[]{:S(2)}, u32[]{:S(2)}) collective-permute-start(bf16[4,64,128]{2,1,0:T(8,128)(2,1)S(1)} %get-tuple-element.97), channel_id=1, source_target_pairs={{0,12},{1,13},{2,14},{3,15},{4,0},{5,1},{6,2},{7,3},{8,4},{9,5},{1... | collective-permute-start | bytes 196616 | tf_op jit(solution)/shard_map/ppermute | solution.py:78
  27.0 3.1 %collective-permute-done.9 = bf16[4,64,128]{2,1,0:T(8,128)(2,1)S(1)} collective-permute-done((bf16[4,64,128]{2,1,0:T(8,128)(2,1)S(1)}, bf16[4,64,128]{2,1,0:T(8,128)(2,1)S(1)}, u32[]{:S(2)}, u32[]{:S(2)}) %collective-permute-start.9) | collective-permute-done | bytes 65568 | tf_op jit(solution)/shard_map/ppermute | solution.py:78
  33.0 3.5 %collective-permute-start.13 = (bf16[4,4,64,128]{3,2,1,0:T(8,128)(2,1)S(1)}, bf16[4,4,64,128]{3,2,1,0:T(8,128)(2,1)S(1)}, u32[]{:S(2)}, u32[]{:S(2)}) collective-permute-start(bf16[4,4,64,128]{3,2,1,0:T(8,128)(2,1)S(1)} %get-tuple-element.94), channel_id=1, source_target_pairs={{0,2},{1,3},{2,0},{3,1},{4,6},{5,7},{6,4},{7,5},{8,10},{9,11},{10,... | collective-permute-start | bytes 786440 | tf_op jit(solution)/shard_map/ppermute | solution.py:78
  37.5 2.7 %collective-permute-done.12 = bf16[4,4,64,128]{3,2,1,0:T(8,128)(2,1)S(1)} collective-permute-done((bf16[4,4,64,128]{3,2,1,0:T(8,128)(2,1)S(1)}, bf16[4,4,64,128]{3,2,1,0:T(8,128)(2,1)S(1)}, u32[]{:S(2)}, u32[]{:S(2)}) %collective-permute-start.12) | collective-permute-done | bytes 262176 | tf_op jit(solution)/shard_map/ppermute | solution.py:78
  40.2 3.4 %collective-permute-done.13 = bf16[4,4,64,128]{3,2,1,0:T(8,128)(2,1)S(1)} collective-permute-done((bf16[4,4,64,128]{3,2,1,0:T(8,128)(2,1)S(1)}, bf16[4,4,64,128]{3,2,1,0:T(8,128)(2,1)S(1)}, u32[]{:S(2)}, u32[]{:S(2)}) %collective-permute-start.13) | collective-permute-done | bytes 262176 | tf_op jit(solution)/shard_map/ppermute | solution.py:78
  46.3 3.4 %prepare.1.table = s32[339]{0:T(512)} custom-call(s32[5]{0:T(128)} %stack.107.place, s32[16,5]{1,0:T(8,128)} %copy.7.lam, s32[16]{0:T(128)} %tile_count.1, s32[16,5]{1,0:T(8,128)} %copy.8.screen), custom_call_target="tpu_custom_call" | custom-call | tf_op jit(solution)/shard_map/prepare/pallas_call | solution.py:64
  50.4 10.7 %fit.1 = bf16[16,9,16,1024]{3,2,1,0:T(8,128)(2,1)S(1)} custom-call(s32[339]{0:T(512)S(1)} %copy-done.2, bf16[2,64,64,128]{3,2,1,0:T(8,128)(2,1)S(1)} %pad_maximum_fusion.same, bf16[2,64,64,128]{3,2,1,0:T(8,128)(2,1)} %collective-permute-done.15.other, bf16[16,5,9,128,128]{4,3,2,1,0:T(8,128)(2,1)} %integrals.1), custom_call_target="tpu_custom_call" | custom-call | flops 3000000000 | bytes 20000000 | tf_op jit(solution)/shard_map/fit/pallas_call | solution.py:153
  61.2 64.1 %all_to_all.5.fitted = bf16[16,9,16,1024]{3,2,1,0:T(8,128)(2,1)S(1)} all-to-all(bf16[16,9,16,1024]{3,2,1,0:T(8,128)(2,1)S(1)} %fit.1), channel_id=1, replica_groups=mesh['pair'=8,'ri'=16] {'ri'}, dimensions={0} | all-to-all | bytes 9437184 | tf_op jit(solution)/shard_map/all_to_all | solution.py:364
  125.3 3.8 %factor.1 = (bf16[1152,3072]{1,0:T(8,128)(2,1)S(1)}, bf16[2048,1152]{1,0:T(8,128)(2,1)S(1)}) custom-call(bf16[144,144]{1,0:T(8,128)(2,1)S(1)} %copy-done.4, bf16[16,9,16,1024]{3,2,1,0:T(8,128)(2,1)S(1)} %all_to_all.5.fitted), custom_call_target="tpu_custom_call" | custom-call | flops 2000000000 | bytes 10000000 | tf_op jit(solution)/shard_map/factor/pallas_call | solution.py:208
  129.1 6.1 %panel_columns.3 = (bf16[4,64,512]{2,1,0:T(8,128)(2,1)S(1)}, bf16[4,64,512]{2,1,0:T(8,128)(2,1)S(1)}, bf16[4,64,512]{2,1,0:T(8,128)(2,1)S(1)}, bf16[4,64,512]{2,...) custom-call(s32[339]{0:T(512)S(1)} %copy-done.3, ...), custom_call_target="tpu_custom_call" | custom-call | flops 3200000000 | bytes 15000000 | tf_op jit(solution)/shard_map/panel_columns/pallas_call | solution.py:252
  137.3 6.3 %panel_columns.2 = (bf16[4,64,640]{2,1,0:T(8,128)(2,1)S(1)}, bf16[4,64,640]{2,1,0:T(8,128)(2,1)S(1)}, bf16[4,64,640]{2,1,0:T(8,128)(2,1)S(1)}, bf16[4,64,640]{2,...) custom-call(s32[339]{0:T(512)S(1)} %copy-done.3, ...), custom_call_target="tpu_custom_call" | custom-call | flops 4000000000 | bytes 15000000 | tf_op jit(solution)/shard_map/panel_columns/pallas_call | solution.py:252
  143.6 2.2 %collective-permute-start.16 = (bf16[4,64,640]{2,1,0:T(8,128)(2,1)S(1)}, bf16[4,64,640]{2,1,0:T(8,128)(2,1)S(1)}, u32[]{:S(2)}, u32[]{:S(2)}) collective-permute-start(bf16[4,64,640]{2,1,0:T(8,128)(2,1)S(1)} %get-tuple-element.51), channel_id=1, source_target_pairs={{0,1},{1,2},{2,3},{3,0},{4,5},{5,6},{6,7},{7,4},{8,9},{9,10},{10,1... | collective-permute-start | bytes 983048 | tf_op jit(solution)/shard_map/ppermute | solution.py:369
  147.3 2.6 %collective-permute-done.28.rest_1_ = bf16[4,64,512]{2,1,0:T(8,128)(2,1)S(1)} collective-permute-done((bf16[4,64,512]{2,1,0:T(8,128)(2,1)S(1)}, bf16[4,64,512]{2,1,0:T(8,128)(2,1)S(1)}, u32[]{:S(2)}, u32[]{:S(2)}) %collective-permute-start.28) | collective-permute-done | bytes 262176 | tf_op jit(solution)/shard_map/ppermute | solution.py:369
  153.0 4.8 %collective-permute-done.31.rest_5_ = bf16[4,64,512]{2,1,0:T(8,128)(2,1)S(1)} collective-permute-done((bf16[4,64,512]{2,1,0:T(8,128)(2,1)S(1)}, bf16[4,64,512]{2,1,0:T(8,128)(2,1)S(1)}, u32[]{:S(2)}, u32[]{:S(2)}) %collective-permute-start.31) | collective-permute-done | bytes 262176 | tf_op jit(solution)/shard_map/ppermute | solution.py:370
  168.3 8.2 %collective-permute-done.19.rest_5_ = bf16[4,64,640]{2,1,0:T(8,128)(2,1)S(1)} collective-permute-done((bf16[4,64,640]{2,1,0:T(8,128)(2,1)S(1)}, bf16[4,64,640]{2,1,0:T(8,128)(2,1)S(1)}, u32[]{:S(2)}, u32[]{:S(2)}) %collective-permute-start.19) | collective-permute-done | bytes 327712 | tf_op jit(solution)/shard_map/ppermute | solution.py:370
  180.9 2.2 %collective-permute-start.39 = (bf16[64,512]{1,0:T(8,128)(2,1)S(1)}, bf16[64,512]{1,0:T(8,128)(2,1)S(1)}, u32[]{:S(2)}, u32[]{:S(2)}) collective-permute-start(bf16[64,512]{1,0:T(8,128)(2,1)S(1)} %get-tuple-element.82), channel_id=1, source_target_pairs={{0,3},{1,0},{2,1},{3,2},{4,7},{5,4},{6,5},{7,6},{8,11},{9,8},{10,9... | collective-permute-start | bytes 196616 | tf_op jit(solution)/shard_map/ppermute | solution.py:370
  183.1 3.5 %collective-permute-start.23 = (bf16[64,640]{1,0:T(8,128)(2,1)S(1)}, bf16[64,640]{1,0:T(8,128)(2,1)S(1)}, u32[]{:S(2)}, u32[]{:S(2)}) collective-permute-start(bf16[64,640]{1,0:T(8,128)(2,1)S(1)} %get-tuple-element.60), channel_id=1, source_target_pairs={{0,8},{1,9},{2,10},{3,11},{4,12},{5,13},{6,14},{7,15},{8,0},{9,1},... | collective-permute-start | bytes 245768 | tf_op jit(solution)/shard_map/ppermute | solution.py:369
  186.7 3.4 %collective-permute-start.26 = (bf16[64,640]{1,0:T(8,128)(2,1)S(1)}, bf16[64,640]{1,0:T(8,128)(2,1)S(1)}, u32[]{:S(2)}, u32[]{:S(2)}) collective-permute-start(bf16[64,640]{1,0:T(8,128)(2,1)S(1)} %get-tuple-element.64), channel_id=1, source_target_pairs={{0,2},{1,3},{2,0},{3,1},{4,6},{5,7},{6,4},{7,5},{8,10},{9,11},{10,... | collective-permute-start | bytes 245768 | tf_op jit(solution)/shard_map/ppermute | solution.py:370
  195.1 3.6 %collective-permute-start.46 = (bf16[128,128]{1,0:T(8,128)(2,1)S(1)}, bf16[128,128]{1,0:T(8,128)(2,1)S(1)}, u32[]{:S(2)}, u32[]{:S(2)}) collective-permute-start(bf16[128,128]{1,0:T(8,128)(2,1)S(1)} %get-tuple-element.90), channel_id=1, source_target_pairs={{0,7},{1,8},{2,9},{3,10},{4,11},{5,12},{6,13},{7,14},{8,15},{9,0},... | collective-permute-start | bytes 98312 | tf_op jit(solution)/shard_map/ppermute | solution.py:384
  199.6 2.7 %collective-permute-start.41 = (bf16[128,128]{1,0:T(8,128)(2,1)S(1)}, bf16[128,128]{1,0:T(8,128)(2,1)S(1)}, u32[]{:S(2)}, u32[]{:S(2)}) collective-permute-start(bf16[128,128]{1,0:T(8,128)(2,1)S(1)} %get-tuple-element.85), channel_id=1, source_target_pairs={{0,2},{1,3},{2,4},{3,5},{4,6},{5,7},{6,8},{7,9},{8,10},{9,11},{10,... | collective-permute-start | bytes 98312 | tf_op jit(solution)/shard_map/ppermute | solution.py:384
  202.3 2.6 %collective-permute-start.42 = (bf16[128,128]{1,0:T(8,128)(2,1)S(1)}, bf16[128,128]{1,0:T(8,128)(2,1)S(1)}, u32[]{:S(2)}, u32[]{:S(2)}) collective-permute-start(bf16[128,128]{1,0:T(8,128)(2,1)S(1)} %get-tuple-element.86), channel_id=1, source_target_pairs={{0,3},{1,4},{2,5},{3,6},{4,7},{5,8},{6,9},{7,10},{8,11},{9,12},{10... | collective-permute-start | bytes 98312 | tf_op jit(solution)/shard_map/ppermute | solution.py:384
  210.6 2.2 %place_blocks.1 = f32[128,2048]{1,0:T(8,128)} custom-call(s32[339]{0:T(512)} %prepare.1.table, f32[128,640]{1,0:T(8,128)} %copy-done, f32[128,512]{1,0:T(8,128)} %copy-done.1, bf16[128,128]{1,0:T(8,128)(2,1)} %copy-done.8, bf16[128,128]{1,0:T(8,128)(2,1)} %copy-done.9, bf16[128,128]{1,0:T(8,128)(2,1)} %copy-done.10, bf16[128,128]{1,0:T(8,128)(2,1)} %copy-done.11, ...), custom_call_target="tpu_custom_call" | custom-call | tf_op jit(solution)/shard_map/place_blocks/pallas_call | solution.py:338
  (119 shorter events, 58.7 us)
Async XLA Ops:
  19.2 17.3 %collective-permute-start.6 = (bf16[4,4,64,128]{3,2,1,0:T(8,128)(2,1)S(1)}, bf16[4,4,64,128]{3,2,1,0:T(8,128)(2,1)S(1)}, u32[]{:S(2)}, u32[]{:S(2)}) collective-permute-start(bf16[4,4,64,128]{3,2,1,0:T(8,128)(2,1)S(1)} %get-tuple-element.92), channel_id=1, source_target_pairs={{0,4},{1,5},{2,6},{3,7},{4,8},{5,9},{6,10},{7,11},{8,12},{9,13},{1... | collective-permute-start | bytes 786440 | tf_op jit(solution)/shard_map/ppermute | solution.py:78
  20.8 9.3 %collective-permute-start.9 = (bf16[4,64,128]{2,1,0:T(8,128)(2,1)S(1)}, bf16[4,64,128]{2,1,0:T(8,128)(2,1)S(1)}, u32[]{:S(2)}, u32[]{:S(2)}) collective-permute-start(bf16[4,64,128]{2,1,0:T(8,128)(2,1)S(1)} %get-tuple-element.97), channel_id=1, source_target_pairs={{0,4},{1,5},{2,6},{3,7},{4,8},{5,9},{6,10},{7,11},{8,12},{9,13},{1... | collective-permute-start | bytes 196616 | tf_op jit(solution)/shard_map/ppermute | solution.py:78
  22.4 10.1 %collective-permute-start.10 = (bf16[4,64,128]{2,1,0:T(8,128)(2,1)S(1)}, bf16[4,64,128]{2,1,0:T(8,128)(2,1)S(1)}, u32[]{:S(2)}, u32[]{:S(2)}) collective-permute-start(bf16[4,64,128]{2,1,0:T(8,128)(2,1)S(1)} %get-tuple-element.97), channel_id=1, source_target_pairs={{0,8},{1,9},{2,10},{3,11},{4,12},{5,13},{6,14},{7,15},{8,0},{9,1},... | collective-permute-start | bytes 196616 | tf_op jit(solution)/shard_map/ppermute | solution.py:78
  26.3 11.0 %collective-permute-start.7 = (bf16[4,4,64,128]{3,2,1,0:T(8,128)(2,1)S(1)}, bf16[4,4,64,128]{3,2,1,0:T(8,128)(2,1)S(1)}, u32[]{:S(2)}, u32[]{:S(2)}) collective-permute-start(bf16[4,4,64,128]{3,2,1,0:T(8,128)(2,1)S(1)} %get-tuple-element.92), channel_id=1, source_target_pairs={{0,8},{1,9},{2,10},{3,11},{4,12},{5,13},{6,14},{7,15},{8,0},{9,1},... | collective-permute-start | bytes 786440 | tf_op jit(solution)/shard_map/ppermute | solution.py:78
  33.0 10.7 %collective-permute-start.13 = (bf16[4,4,64,128]{3,2,1,0:T(8,128)(2,1)S(1)}, bf16[4,4,64,128]{3,2,1,0:T(8,128)(2,1)S(1)}, u32[]{:S(2)}, u32[]{:S(2)}) collective-permute-start(bf16[4,4,64,128]{3,2,1,0:T(8,128)(2,1)S(1)} %get-tuple-element.94), channel_id=1, source_target_pairs={{0,2},{1,3},{2,0},{3,1},{4,6},{5,7},{6,4},{7,5},{8,10},{9,11},{10,... | collective-permute-start | bytes 786440 | tf_op jit(solution)/shard_map/ppermute | solution.py:78
  135.2 14.7 %collective-permute-start.28 = (bf16[4,64,512]{2,1,0:T(8,128)(2,1)S(1)}, bf16[4,64,512]{2,1,0:T(8,128)(2,1)S(1)}, u32[]{:S(2)}, u32[]{:S(2)}) collective-permute-start(bf16[4,64,512]{2,1,0:T(8,128)(2,1)S(1)} %get-tuple-element.68), channel_id=1, source_target_pairs={{0,1},{1,2},{2,3},{3,0},{4,5},{5,6},{6,7},{7,4},{8,9},{9,10},{10,1... | collective-permute-start | bytes 786440 | tf_op jit(solution)/shard_map/ppermute | solution.py:369
  135.8 14.0 %collective-permute-start.29 = (bf16[4,64,512]{2,1,0:T(8,128)(2,1)S(1)}, bf16[4,64,512]{2,1,0:T(8,128)(2,1)S(1)}, u32[]{:S(2)}, u32[]{:S(2)}) collective-permute-start(bf16[4,64,512]{2,1,0:T(8,128)(2,1)S(1)} %get-tuple-element.69), channel_id=1, source_target_pairs={{0,2},{1,3},{2,0},{3,1},{4,6},{5,7},{6,4},{7,5},{8,10},{9,11},{10,... | collective-permute-start | bytes 786440 | tf_op jit(solution)/shard_map/ppermute | solution.py:369
  143.6 19.3 %collective-permute-start.16 = (bf16[4,64,640]{2,1,0:T(8,128)(2,1)S(1)}, bf16[4,64,640]{2,1,0:T(8,128)(2,1)S(1)}, u32[]{:S(2)}, u32[]{:S(2)}) collective-permute-start(bf16[4,64,640]{2,1,0:T(8,128)(2,1)S(1)} %get-tuple-element.51), channel_id=1, source_target_pairs={{0,1},{1,2},{2,3},{3,0},{4,5},{5,6},{6,7},{7,4},{8,9},{9,10},{10,1... | collective-permute-start | bytes 983048 | tf_op jit(solution)/shard_map/ppermute | solution.py:369
  146.9 10.9 %collective-permute-start.31 = (bf16[4,64,512]{2,1,0:T(8,128)(2,1)S(1)}, bf16[4,64,512]{2,1,0:T(8,128)(2,1)S(1)}, u32[]{:S(2)}, u32[]{:S(2)}) collective-permute-start(bf16[4,64,512]{2,1,0:T(8,128)(2,1)S(1)} %get-tuple-element.72), channel_id=1, source_target_pairs={{0,4},{1,5},{2,6},{3,7},{4,8},{5,9},{6,10},{7,11},{8,12},{9,13},{1... | collective-permute-start | bytes 786440 | tf_op jit(solution)/shard_map/ppermute | solution.py:370
  149.9 11.0 %collective-permute-start.32 = (bf16[4,64,512]{2,1,0:T(8,128)(2,1)S(1)}, bf16[4,64,512]{2,1,0:T(8,128)(2,1)S(1)}, u32[]{:S(2)}, u32[]{:S(2)}) collective-permute-start(bf16[4,64,512]{2,1,0:T(8,128)(2,1)S(1)} %get-tuple-element.73), channel_id=1, source_target_pairs={{0,8},{1,9},{2,10},{3,11},{4,12},{5,13},{6,14},{7,15},{8,0},{9,1},... | collective-permute-start | bytes 786440 | tf_op jit(solution)/shard_map/ppermute | solution.py:370
  149.9 11.0 %collective-permute-start.33 = (bf16[4,64,512]{2,1,0:T(8,128)(2,1)S(1)}, bf16[4,64,512]{2,1,0:T(8,128)(2,1)S(1)}, u32[]{:S(2)}, u32[]{:S(2)}) collective-permute-start(bf16[4,64,512]{2,1,0:T(8,128)(2,1)S(1)} %get-tuple-element.74), channel_id=1, source_target_pairs={{0,12},{1,13},{2,14},{3,15},{4,0},{5,1},{6,2},{7,3},{8,4},{9,5},{1... | collective-permute-start | bytes 786440 | tf_op jit(solution)/shard_map/ppermute | solution.py:370
  152.1 12.9 %collective-permute-start.17 = (bf16[4,64,640]{2,1,0:T(8,128)(2,1)S(1)}, bf16[4,64,640]{2,1,0:T(8,128)(2,1)S(1)}, u32[]{:S(2)}, u32[]{:S(2)}) collective-permute-start(bf16[4,64,640]{2,1,0:T(8,128)(2,1)S(1)} %get-tuple-element.52), channel_id=1, source_target_pairs={{0,2},{1,3},{2,0},{3,1},{4,6},{5,7},{6,4},{7,5},{8,10},{9,11},{10,... | collective-permute-start | bytes 983048 | tf_op jit(solution)/shard_map/ppermute | solution.py:369
  160.9 15.7 %collective-permute-start.19 = (bf16[4,64,640]{2,1,0:T(8,128)(2,1)S(1)}, bf16[4,64,640]{2,1,0:T(8,128)(2,1)S(1)}, u32[]{:S(2)}, u32[]{:S(2)}) collective-permute-start(bf16[4,64,640]{2,1,0:T(8,128)(2,1)S(1)} %get-tuple-element.55), channel_id=1, source_target_pairs={{0,4},{1,5},{2,6},{3,7},{4,8},{5,9},{6,10},{7,11},{8,12},{9,13},{1... | collective-permute-start | bytes 983048 | tf_op jit(solution)/shard_map/ppermute | solution.py:370
  160.9 15.7 %collective-permute-start.20 = (bf16[4,64,640]{2,1,0:T(8,128)(2,1)S(1)}, bf16[4,64,640]{2,1,0:T(8,128)(2,1)S(1)}, u32[]{:S(2)}, u32[]{:S(2)}) collective-permute-start(bf16[4,64,640]{2,1,0:T(8,128)(2,1)S(1)} %get-tuple-element.56), channel_id=1, source_target_pairs={{0,8},{1,9},{2,10},{3,11},{4,12},{5,13},{6,14},{7,15},{8,0},{9,1},... | collective-permute-start | bytes 983048 | tf_op jit(solution)/shard_map/ppermute | solution.py:370
  162.9 15.1 %collective-permute-start.21 = (bf16[4,64,640]{2,1,0:T(8,128)(2,1)S(1)}, bf16[4,64,640]{2,1,0:T(8,128)(2,1)S(1)}, u32[]{:S(2)}, u32[]{:S(2)}) collective-permute-start(bf16[4,64,640]{2,1,0:T(8,128)(2,1)S(1)} %get-tuple-element.57), channel_id=1, source_target_pairs={{0,12},{1,13},{2,14},{3,15},{4,0},{5,1},{6,2},{7,3},{8,4},{9,5},{1... | collective-permute-start | bytes 983048 | tf_op jit(solution)/shard_map/ppermute | solution.py:370
  165.0 14.8 %collective-permute-start.34 = (bf16[64,512]{1,0:T(8,128)(2,1)S(1)}, bf16[64,512]{1,0:T(8,128)(2,1)S(1)}, u32[]{:S(2)}, u32[]{:S(2)}) collective-permute-start(bf16[64,512]{1,0:T(8,128)(2,1)S(1)} %get-tuple-element.76), channel_id=1, source_target_pairs={{0,4},{1,5},{2,6},{3,7},{4,8},{5,9},{6,10},{7,11},{8,12},{9,13},{1... | collective-permute-start | bytes 196616 | tf_op jit(solution)/shard_map/ppermute | solution.py:369
  166.5 14.4 %collective-permute-start.35 = (bf16[64,512]{1,0:T(8,128)(2,1)S(1)}, bf16[64,512]{1,0:T(8,128)(2,1)S(1)}, u32[]{:S(2)}, u32[]{:S(2)}) collective-permute-start(bf16[64,512]{1,0:T(8,128)(2,1)S(1)} %get-tuple-element.77), channel_id=1, source_target_pairs={{0,8},{1,9},{2,10},{3,11},{4,12},{5,13},{6,14},{7,15},{8,0},{9,1},... | collective-permute-start | bytes 196616 | tf_op jit(solution)/shard_map/ppermute | solution.py:369
  176.5 10.0 %collective-permute-start.37 = (bf16[64,512]{1,0:T(8,128)(2,1)S(1)}, bf16[64,512]{1,0:T(8,128)(2,1)S(1)}, u32[]{:S(2)}, u32[]{:S(2)}) collective-permute-start(bf16[64,512]{1,0:T(8,128)(2,1)S(1)} %get-tuple-element.80), channel_id=1, source_target_pairs={{0,1},{1,2},{2,3},{3,0},{4,5},{5,6},{6,7},{7,4},{8,9},{9,10},{10,1... | collective-permute-start | bytes 196616 | tf_op jit(solution)/shard_map/ppermute | solution.py:370
  178.8 11.3 %collective-permute-start.22 = (bf16[64,640]{1,0:T(8,128)(2,1)S(1)}, bf16[64,640]{1,0:T(8,128)(2,1)S(1)}, u32[]{:S(2)}, u32[]{:S(2)}) collective-permute-start(bf16[64,640]{1,0:T(8,128)(2,1)S(1)} %get-tuple-element.59), channel_id=1, source_target_pairs={{0,4},{1,5},{2,6},{3,7},{4,8},{5,9},{6,10},{7,11},{8,12},{9,13},{1... | collective-permute-start | bytes 245768 | tf_op jit(solution)/shard_map/ppermute | solution.py:369
  183.1 8.8 %collective-permute-start.23 = (bf16[64,640]{1,0:T(8,128)(2,1)S(1)}, bf16[64,640]{1,0:T(8,128)(2,1)S(1)}, u32[]{:S(2)}, u32[]{:S(2)}) collective-permute-start(bf16[64,640]{1,0:T(8,128)(2,1)S(1)} %get-tuple-element.60), channel_id=1, source_target_pairs={{0,8},{1,9},{2,10},{3,11},{4,12},{5,13},{6,14},{7,15},{8,0},{9,1},... | collective-permute-start | bytes 245768 | tf_op jit(solution)/shard_map/ppermute | solution.py:369
  186.7 12.0 %collective-permute-start.26 = (bf16[64,640]{1,0:T(8,128)(2,1)S(1)}, bf16[64,640]{1,0:T(8,128)(2,1)S(1)}, u32[]{:S(2)}, u32[]{:S(2)}) collective-permute-start(bf16[64,640]{1,0:T(8,128)(2,1)S(1)} %get-tuple-element.64), channel_id=1, source_target_pairs={{0,2},{1,3},{2,0},{3,1},{4,6},{5,7},{6,4},{7,5},{8,10},{9,11},{10,... | collective-permute-start | bytes 245768 | tf_op jit(solution)/shard_map/ppermute | solution.py:370
  192.0 10.3 %collective-permute-start.44 = (bf16[128,128]{1,0:T(8,128)(2,1)S(1)}, bf16[128,128]{1,0:T(8,128)(2,1)S(1)}, u32[]{:S(2)}, u32[]{:S(2)}) collective-permute-start(bf16[128,128]{1,0:T(8,128)(2,1)S(1)} %get-tuple-element.88), channel_id=1, source_target_pairs={{0,5},{1,6},{2,7},{3,8},{4,9},{5,10},{6,11},{7,12},{8,13},{9,14},{... | collective-permute-start | bytes 98312 | tf_op jit(solution)/shard_map/ppermute | solution.py:384
  193.0 11.9 %collective-permute-start.45 = (bf16[128,128]{1,0:T(8,128)(2,1)S(1)}, bf16[128,128]{1,0:T(8,128)(2,1)S(1)}, u32[]{:S(2)}, u32[]{:S(2)}) collective-permute-start(bf16[128,128]{1,0:T(8,128)(2,1)S(1)} %get-tuple-element.89), channel_id=1, source_target_pairs={{0,6},{1,7},{2,8},{3,9},{4,10},{5,11},{6,12},{7,13},{8,14},{9,15},... | collective-permute-start | bytes 98312 | tf_op jit(solution)/shard_map/ppermute | solution.py:384
  195.1 10.0 %collective-permute-start.46 = (bf16[128,128]{1,0:T(8,128)(2,1)S(1)}, bf16[128,128]{1,0:T(8,128)(2,1)S(1)}, u32[]{:S(2)}, u32[]{:S(2)}) collective-permute-start(bf16[128,128]{1,0:T(8,128)(2,1)S(1)} %get-tuple-element.90), channel_id=1, source_target_pairs={{0,7},{1,8},{2,9},{3,10},{4,11},{5,12},{6,13},{7,14},{8,15},{9,0},... | collective-permute-start | bytes 98312 | tf_op jit(solution)/shard_map/ppermute | solution.py:384
  (37 other events, 300.1 us)
